TPU v7x, 256 devices: a whole 4x4x8 slice. The times are simulated.
256 devices in a mesh: row: 32 (over z, y_hi, core), col: 8 (over x, y_lo).
Axes of the slice: x: 4, y: 4 (y_hi: 2, y_lo: 2; y = y_hi * 2 + y_lo), z: 8, core: 2. Of those that a mesh axis runs over, the one named last changes fastest.
Arguments:
- rewards: float32 [16384, 512], P(('row', 'col')), as said below
- tile_data: bfloat16 [32, 8, 12, 256, 256], P('row', 'col'), as said below
- tile_slots: int32 [32, 8, 12], P('row', 'col'), may hold values from 0 to 15, as said below
- tile_count: int32 [32, 8], P('row', 'col'), may hold values from 6 to 12, as said below
Outputs:
- estimate: float32 [16384, 512], P(('row', 'col'))
- relative_residual: float32 [512], replicated
Inputs may be any that keep to these rules, and one draw needn't show every extreme that they name: rewards have a scale per state and a scale per channel. `tile_data`: entries are nonnegative; every row of P sums to at most 1. `tile_slots`: in every block, slot s lies in tile row (s + a start drawn per block) mod 2. `tile_count`: some block has all 12 slots live.
All inputs are finite; a program needn't handle non-finite values.
Results may differ from a plain program's by a relative error of at most 0.00043.
Values may be sent and summed in bfloat16 or wider, within the bound.
No kernel may reach another device: no remote copies, remote signals or barrier semaphores. Data moves between devices by JAX's collectives and lax.ppermute only.
A program may use at most 128 MiB of HBM per device.

v0:
```python
import jax
import jax.numpy as jnp
from jax import lax
from jax.sharding import PartitionSpec as P

ITERS = 2


EPS = 1e-06
GAMMA = 0.9


def forward_part(tile_data, tile_slots, tile_count, values_block, tile_rows):
    n_slots = tile_data.shape[0]
    tile_size = tile_data.shape[-1]
    tile_cols = values_block.shape[0] // tile_size
    pieces = values_block.reshape(tile_cols, tile_size, -1)[tile_slots % tile_cols]
    products = jnp.einsum("sij,sjk->sik", tile_data, pieces, preferred_element_type=jnp.float32)
    live_mask = (jnp.arange(n_slots, dtype=jnp.int32) < tile_count).astype(jnp.float32)
    placing = (
        tile_slots[None, :] // tile_cols == jnp.arange(tile_rows, dtype=jnp.int32)[:, None]
    ).astype(jnp.float32) * live_mask[None, :]
    return jnp.einsum("ts,sik->tik", placing, products, precision=lax.Precision.HIGHEST).reshape(
        tile_rows * tile_size, -1
    )


def backward_part(tile_data, tile_slots, tile_count, values_block, tile_cols):
    n_slots = tile_data.shape[0]
    tile_size = tile_data.shape[-1]
    tile_rows = values_block.shape[0] // tile_size
    pieces = values_block.reshape(tile_rows, tile_size, -1)[tile_slots // tile_cols]
    products = jnp.einsum("sij,sik->sjk", tile_data, pieces, preferred_element_type=jnp.float32)
    live_mask = (jnp.arange(n_slots, dtype=jnp.int32) < tile_count).astype(jnp.float32)
    placing = (
        tile_slots[None, :] % tile_cols == jnp.arange(tile_cols, dtype=jnp.int32)[:, None]
    ).astype(jnp.float32) * live_mask[None, :]
    return jnp.einsum("ts,sjk->tjk", placing, products, precision=lax.Precision.HIGHEST).reshape(
        tile_cols * tile_size, -1
    )


def shards(rewards, tile_data, tile_slots, tile_count):
    tile_data = tile_data[0, 0]
    tile_slots = tile_slots[0, 0]
    tile_count = tile_count[0, 0]
    rows_dev = rewards.shape[0]
    tile_size = tile_data.shape[-1]
    tile_rows = lax.axis_size("col") * rows_dev // tile_size
    tile_cols = lax.axis_size("row") * rows_dev // tile_size
    my_row = lax.axis_index("row")

    def norm_all(values):
        summed = lax.psum(jnp.sum(values * values, axis=0), ("row", "col"))
        return jnp.sqrt(summed + EPS)

    def adjoint_terms(left_vec):
        gathered = lax.all_gather(left_vec.astype(jnp.bfloat16), "col", axis=0, tiled=True)
        partials = -GAMMA * backward_part(tile_data, tile_slots, tile_count, gathered, tile_cols)
        own_rows = lax.dynamic_slice_in_dim(partials, my_row * rows_dev, rows_dev, 0) + left_vec
        return lax.dynamic_update_slice_in_dim(partials, own_rows, my_row * rows_dev, 0)

    def adjoint_scatter(left_vec, right_prev, beta_val):
        summed = lax.psum_scatter(adjoint_terms(left_vec), "row", scatter_dimension=0, tiled=True)
        raw_vec = summed if right_prev is None else summed - beta_val * right_prev
        alpha_val = norm_all(raw_vec)
        return (raw_vec / alpha_val, alpha_val)

    beta_val = norm_all(rewards)
    beta_first = beta_val
    left_vec = rewards / beta_val
    right_vec, alpha_val = adjoint_scatter(left_vec, None, beta_val)
    direction = right_vec
    estimate = jnp.zeros_like(rewards)
    phibar = beta_val
    rhobar = alpha_val
    for iteration in range(ITERS):
        gathered = lax.all_gather(right_vec.astype(jnp.bfloat16), "row", axis=0, tiled=True)
        apply_partials = forward_part(tile_data, tile_slots, tile_count, gathered, tile_rows)
        apply_summed = lax.psum_scatter(apply_partials, "col", scatter_dimension=0, tiled=True)
        left_vec = right_vec - GAMMA * apply_summed - alpha_val * left_vec
        beta_val = norm_all(left_vec)
        left_vec = left_vec / beta_val
        right_vec, alpha_val = adjoint_scatter(left_vec, right_vec, beta_val)
        rho_val = jnp.sqrt(rhobar * rhobar + beta_val * beta_val)
        cosine = rhobar / rho_val
        sine_val = beta_val / rho_val
        theta_val = sine_val * alpha_val
        rhobar = -cosine * alpha_val
        phi_val = cosine * phibar
        phibar = sine_val * phibar
        estimate = estimate + phi_val / rho_val * direction
        direction = right_vec - theta_val / rho_val * direction
    return (estimate, phibar / beta_first)


def solution(mesh):
    return jax.shard_map(
        shards,
        mesh=mesh,
        in_specs=(
            P(("row", "col"), None),
            P("row", "col", None, None, None),
            P("row", "col", None),
            P("row", "col"),
        ),
        out_specs=(P(("row", "col"), None), P()),
        check_vma=False,
    )
```

profile of v0, /device:TPU:1, one launch (start us, length us, event | category | flops | bytes accessed | tf_op | source)
XLA Modules:
  0.0 1055.7 jit_solution(16255891721491420121)
XLA Ops:
  10.3 81.4 %psum.35 = f32[512]{0:T(512)S(1)} all-reduce(f32[512]{0:T(512)S(1)} %multiply_reduce_fusion.4), channel_id=1, replica_groups=mesh['row'=32,'col'=8] {'row','col'}, use_global_device_ids=true, to_apply=%region_1.0 | all-reduce | flops 512 | bytes 4096 | tf_op jit(solution)/shard_map/psum | solution.py:54
  92.6 23.2 %all_gather.12 = bf16[512,512]{1,0:T(8,128)(2,1)S(1)} all-gather(bf16[64,512]{1,0:T(8,128)(2,1)S(1)} %fusion.49), channel_id=1, replica_groups=mesh['row'=32,'col'=8] {'col'}, dimensions={0}, use_global_device_ids=true | all-gather | bytes 589824 | tf_op jit(solution)/shard_map/all_gather | solution.py:58
  115.9 2.5 gather_fusion
  118.4 5.7 fusion.20
  124.1 9.7 copy.10
  133.8 6.7 fusion.8
  140.5 4.4 copy.6
  144.8 1.6 add_dynamic-update-slice_fusion.1
  146.5 123.5 %reduce-scatter.5.cloned.1.call-done = f32[64,512]{1,0:T(8,128)} async-done(((f32[2048,512]{1,0:T(8,128)}), f32[64,512]{1,0:T(8,128)}) %reduce-scatter.5.cloned.1.call-update) | async-done | bytes 131088 | tf_op jit(solution)/shard_map/reduce_scatter | solution.py:64
  270.9 79.1 %psum.36 = f32[512]{0:T(512)S(1)} all-reduce(f32[512]{0:T(512)S(1)} %multiply_reduce_fusion.3), channel_id=1, replica_groups=mesh['row'=32,'col'=8] {'row','col'}, use_global_device_ids=true, to_apply=%region_4.5 | all-reduce | flops 512 | bytes 4096 | tf_op jit(solution)/shard_map/psum | solution.py:54
  351.9 76.6 %all-gather.3.cloned.1.call-done = bf16[2048,512]{1,0:T(8,128)(2,1)} async-done(((bf16[64,512]{1,0:T(8,128)(2,1)}), bf16[2048,512]{1,0:T(8,128)(2,1)}) %all-gather.3.cloned.1.call-update) | async-done | bytes 2097168 | tf_op jit(solution)/shard_map/all_gather | solution.py:78
  428.5 4.1 gather_fusion.1
  432.6 5.7 fusion.18
  438.3 9.7 copy.11
  448.0 6.4 fusion.4
  455.6 33.7 %reduce-scatter.7.cloned.1.call-done = f32[64,512]{1,0:T(8,128)} async-done(((f32[512,512]{1,0:T(8,128)}), f32[64,512]{1,0:T(8,128)}) %reduce-scatter.7.cloned.1.call-update) | async-done | bytes 131088 | tf_op jit(solution)/shard_map/reduce_scatter | solution.py:80
  490.3 78.4 %psum.37 = f32[512]{0:T(512)S(1)} all-reduce(f32[512]{0:T(512)S(1)} %get-tuple-element.2), channel_id=1, replica_groups=mesh['row'=32,'col'=8] {'row','col'}, use_global_device_ids=true, to_apply=%region_7.8 | all-reduce | flops 512 | bytes 4096 | tf_op jit(solution)/shard_map/psum | solution.py:54
  568.8 23.2 %all_gather.14 = bf16[512,512]{1,0:T(8,128)(2,1)S(1)} all-gather(bf16[64,512]{1,0:T(8,128)(2,1)S(1)} %fusion.50), channel_id=1, replica_groups=mesh['row'=32,'col'=8] {'col'}, dimensions={0}, use_global_device_ids=true | all-gather | bytes 589824 | tf_op jit(solution)/shard_map/all_gather | solution.py:58
  592.0 2.5 gather_fusion.2
  594.5 5.7 fusion.16
  600.2 9.7 copy.12
  609.9 6.7 fusion.11
  616.6 4.4 copy.8
  622.6 125.7 %reduce-scatter.9.cloned.1.call-done = f32[64,512]{1,0:T(8,128)} async-done(((f32[2048,512]{1,0:T(8,128)}), f32[64,512]{1,0:T(8,128)}) %reduce-scatter.9.cloned.1.call-update) | async-done | bytes 131088 | tf_op jit(solution)/shard_map/reduce_scatter | solution.py:64
  749.3 79.5 %psum.38 = f32[512]{0:T(512)S(1)} all-reduce(f32[512]{0:T(512)S(1)} %multiply_reduce_fusion.1), channel_id=1, replica_groups=mesh['row'=32,'col'=8] {'row','col'}, use_global_device_ids=true, to_apply=%region_10.11 | all-reduce | flops 512 | bytes 4096 | tf_op jit(solution)/shard_map/psum | solution.py:54
  830.7 76.5 %all-gather.5.cloned.1.call-done = bf16[2048,512]{1,0:T(8,128)(2,1)} async-done(((bf16[64,512]{1,0:T(8,128)(2,1)}), bf16[2048,512]{1,0:T(8,128)(2,1)}) %all-gather.5.cloned.1.call-update) | async-done | bytes 2097168 | tf_op jit(solution)/shard_map/all_gather | solution.py:78
  907.2 4.1 gather_fusion.3
  911.4 5.7 fusion.14
  917.1 9.7 copy.13
  926.7 6.4 fusion
  934.4 33.9 %reduce-scatter.11.cloned.1.call-done = f32[64,512]{1,0:T(8,128)} async-done(((f32[512,512]{1,0:T(8,128)}), f32[64,512]{1,0:T(8,128)}) %reduce-scatter.11.cloned.1.call-update) | async-done | bytes 131088 | tf_op jit(solution)/shard_map/reduce_scatter | solution.py:80
  969.3 78.2 %psum.39 = f32[512]{0:T(512)S(1)} all-reduce(f32[512]{0:T(512)S(1)} %multiply_reduce_fusion), channel_id=1, replica_groups=mesh['row'=32,'col'=8] {'row','col'}, use_global_device_ids=true, to_apply=%region_13.14 | all-reduce | flops 512 | bytes 4096 | tf_op jit(solution)/shard_map/psum | solution.py:54
  (43 shorter events, 16.4 us)
Async XLA Ops:
  7.2 111.2 %copy-start = (bf16[1,1,12,256,256]{4,3,2,1,0:T(8,128)(2,1)S(1)}, bf16[1,1,12,256,256]{4,3,2,1,0:T(8,128)(2,1)}, u32[]{:S(2)}) copy-start(bf16[1,1,12,256,256]{4,3,2,1,0:T(8,128)(2,1)} %param.5) | copy-start | bytes 4718596
  7.2 262.8 %reduce-scatter.5.cloned.1.call-start = ((), (), s32[]{:S(2)}) async-start(), calls=%async_computation.4 | async-start | bytes 4325376 | tf_op jit(solution)/shard_map/reduce_scatter | solution.py:64
  140.5 4.4 copy-start.2
  146.4 282.0 %all-gather.3.cloned.1.call-start = ((), (), s32[]{:S(2)}) async-start(), calls=%async_computation.5 | async-start | bytes 2162688 | tf_op jit(solution)/shard_map/all_gather | solution.py:78
  351.6 137.7 %reduce-scatter.7.cloned.1.call-start = ((), (), s32[]{:S(2)}) async-start(), calls=%async_computation.6 | async-start | bytes 1179648 | tf_op jit(solution)/shard_map/reduce_scatter | solution.py:80
  454.4 35.0 %copy-start.1 = (f32[64,512]{1,0:T(8,128)S(1)}, f32[64,512]{1,0:T(8,128)}, u32[]{:S(2)}) copy-start(f32[64,512]{1,0:T(8,128)} %reduce-scatter.5.cloned.1.call-done) | copy-start | bytes 393220
  455.6 292.7 %reduce-scatter.9.cloned.1.call-start = ((), (), s32[]{:S(2)}) async-start(), calls=%async_computation.7 | async-start | bytes 4325376 | tf_op jit(solution)/shard_map/reduce_scatter | solution.py:64
  622.6 284.7 %all-gather.5.cloned.1.call-start = ((), (), s32[]{:S(2)}) async-start(), calls=%async_computation.8 | async-start | bytes 2162688 | tf_op jit(solution)/shard_map/all_gather | solution.py:78
  830.4 137.9 %reduce-scatter.11.cloned.1.call-start = ((), (), s32[]{:S(2)}) async-start(), calls=%async_computation.9 | async-start | bytes 1179648 | tf_op jit(solution)/shard_map/reduce_scatter | solution.py:80
  933.1 35.1 %copy-start.3 = (f32[64,512]{1,0:T(8,128)S(1)}, f32[64,512]{1,0:T(8,128)}, u32[]{:S(2)}) copy-start(f32[64,512]{1,0:T(8,128)} %reduce-scatter.9.cloned.1.call-done) | copy-start | bytes 393220
Sparse Core Ops, SparseCore 0:
  146.5 123.4 reduce-scatter.4
  351.7 76.6 all-gather.2
  455.7 33.6 reduce-scatter.6
  622.7 125.5 reduce-scatter.8
  830.5 76.6 all-gather.4
  934.5 33.7 reduce-scatter.10
where the time goes:
time: 1060 us
  waiting for transfers between devices  470 us (44%)
  blocking collectives  443 us (42%)
  local copies, waits for them, and re-layouts  63.1 us (6%)
  matrix products  49 us (5%)
  between operations  14.9 us (1%)
  other arithmetic  14.8 us (1%)
    psum x5, blocking collectives, norm_all(): summed = lax.psum(jnp.sum(values * values, axis=0), ('row', 'col'))  397 us
    reduce_scatter x2, waiting for transfers between devices, adjoint_scatter(): lax.psum_scatter(adjoint_terms(left_vec), 'row', scatter_dimension=0, til...  249 us
    all_gather x2, waiting for transfers between devices, shards(): lax.all_gather(right_vec.astype(jnp.bfloat16), 'row', axis=0, tiled=True)  153 us
    reduce_scatter x2, waiting for transfers between devices, shards(): lax.psum_scatter(apply_partials, 'col', scatter_dimension=0, tiled=True)  67.6 us
    all_gather x2, blocking collectives, adjoint_terms(): lax.all_gather(left_vec.astype(jnp.bfloat16), 'col', axis=0, tiled=True)  46.5 us
  transfers between devices with their start and end apart: 6, of which 6 were waited for; matrix products, arithmetic and copies ran while one was open for 0% of the time, Pallas kernels for 0%

commit v1 on v0

v1 whole, which is shorter than its diff:
```python
import functools

import jax
import jax.numpy as jnp
import numpy as np
from jax import lax
from jax.experimental import pallas as pl
from jax.experimental.pallas import tpu as pltpu
from jax.sharding import Mesh, PartitionSpec as P

ITERS = 2
EPS = 1e-06
GAMMA = 0.9

AXES = ("z", "yh", "core", "x", "yl")
SIZES = (8, 2, 2, 4, 2)
ROWS = ("z", "yh")
COLS = ("x", "yl")
N_ROWS = 16
N_COLS = 8
TILE = 256
STATES_DEV = 64
PAIR = 2 * STATES_DEV
CHANS = 256
SLOTS = 12
TILE_COLS = 8
HEAD = 16
MSG = PAIR + HEAD
BITS = 14.0
BF16 = jnp.bfloat16
F32 = jnp.float32
I16 = jnp.int16


def to_i16(values):
    return values.astype(jnp.int32).astype(I16)


def scaled_exponent(largest):
    return jnp.ceil(jnp.log2(jnp.maximum(largest, 1e-30)))


def head_rows(exponent, square):
    square_exp = scaled_exponent(square)
    mantissa = square * jnp.exp2(-square_exp) * 16384.0
    high = jnp.round(mantissa)
    low = jnp.round((mantissa - high) * 16384.0)
    row = lax.broadcasted_iota(jnp.int32, (HEAD, exponent.shape[-1]), 0)
    rows = jnp.where(row == 0, exponent, jnp.where(row == 1, square_exp, jnp.where(row == 2, high, low)))
    return to_i16(rows)


def read_head(head):
    rows = head.astype(jnp.int32).astype(F32)
    step = jnp.exp2(rows[0:1] - BITS)
    square = (rows[2:3] + rows[3:4] * (1.0 / 16384.0)) * (1.0 / 16384.0) * jnp.exp2(rows[1:2])
    return step, square


def quantized(block):
    exponent = scaled_exponent(jnp.max(jnp.abs(block), axis=0, keepdims=True))
    return to_i16(jnp.round(block * jnp.exp2(BITS - exponent))), exponent


def store_message(out_ref, block, square):
    values, exponent = quantized(block)
    head = head_rows(exponent, square)
    for i in range(out_ref.shape[0]):
        out_ref[i, :PAIR, :] = values
        out_ref[i, PAIR:, :] = head


def wide(values):
    return values.astype(jnp.int32).astype(F32)


def split_store(ref, index, rows, values):
    high = values.astype(BF16)
    ref[index, rows, :CHANS] = high
    ref[index, rows, CHANS:] = (values - high.astype(F32)).astype(BF16)


def forward_kernel(meta_ref, msg_ref, own_ref, other_ref, out_ref, vec_ref, sum_ref):
    square = jnp.zeros((1, CHANS), F32)
    for k in range(N_ROWS):
        step, part = read_head(msg_ref[k, PAIR:, :])
        square = square + part
        split_store(vec_ref, k // 2, pl.ds((k % 2) * PAIR, PAIR), wide(msg_ref[k, :PAIR, :]) * step)
    core = meta_ref[2, 0]
    for which, tiles_ref in enumerate((own_ref, other_ref)):
        at_core = core if which == 0 else 1 - core
        count = meta_ref[which, SLOTS]
        start = meta_ref[which, 0] // TILE_COLS
        for parity in range(2):
            total = jnp.zeros((TILE, 2 * CHANS), F32)
            for s in range(parity, SLOTS, 2):
                live = jnp.where(s < count, 1.0, 0.0).astype(F32)
                vec = vec_ref[meta_ref[which, s] % TILE_COLS]
                total = total + live * jnp.dot(tiles_ref[s], vec, preferred_element_type=F32)
            tile_row = (start + parity) % 2
            summed = total[:, :CHANS] + total[:, CHANS:]
            for q in range(4):
                sum_ref[tile_row * 4 + q, pl.ds(at_core * STATES_DEV, STATES_DEV), :] = summed[
                    q * STATES_DEV : (q + 1) * STATES_DEV
                ]
    for k in range(N_COLS):
        values, exponent = quantized(sum_ref[k])
        out_ref[k, :PAIR, :] = values
        out_ref[k, PAIR:, :] = head_rows(exponent, square)


def adjoint_kernel(meta_ref, msg_ref, own_ref, other_ref, out_ref, vec_ref, sum_ref):
    square = jnp.zeros((1, CHANS), F32)
    for k in range(N_COLS):
        step, part = read_head(msg_ref[k, PAIR:, :])
        square = square + part
        for core in range(2):
            values = wide(msg_ref[k, core * STATES_DEV : (core + 1) * STATES_DEV, :]) * step
            split_store(vec_ref, core * 2 + k // 4, pl.ds((k % 4) * STATES_DEV, STATES_DEV), values)
    sum_ref[...] = jnp.zeros_like(sum_ref)
    core = meta_ref[2, 0]
    for which, tiles_ref in enumerate((own_ref, other_ref)):
        at_core = core if which == 0 else 1 - core
        count = meta_ref[which, SLOTS]
        for s in range(SLOTS):
            slot = meta_ref[which, s]

            @pl.when(s < count)
            def _():
                vec = vec_ref[at_core * 2 + slot // TILE_COLS]
                product = lax.dot_general(
                    tiles_ref[s], vec, (((0,), (0,)), ((), ())), preferred_element_type=F32
                )
                sum_ref[slot % TILE_COLS] += product[:, :CHANS] + product[:, CHANS:]

    for k in range(N_ROWS):
        values, exponent = quantized(sum_ref[k // 2, (k % 2) * PAIR : (k % 2 + 1) * PAIR, :])
        out_ref[k, :PAIR, :] = values
        out_ref[k, PAIR:, :] = head_rows(exponent, square)


def summed_messages(msg_ref):
    total = jnp.zeros((PAIR, CHANS), F32)
    square = jnp.zeros((1, CHANS), F32)
    for k in range(msg_ref.shape[0]):
        step, part = read_head(msg_ref[k, PAIR:, :])
        total = total + wide(msg_ref[k, :PAIR, :]) * step
        square = square + part
    return total, square


def first_kernel(rewards_ref, out_ref):
    rewards = rewards_ref[...]
    store_message(out_ref, rewards, jnp.sum(rewards * rewards, axis=0, keepdims=True))


def adjoint_end_kernel(first, msg_ref, left_ref, *refs):
    right_ref, (raw_ref, unit_ref, norm_ref, out_ref) = (None, refs) if first else (refs[0], refs[1:])
    total, square = summed_messages(msg_ref)
    beta = jnp.sqrt(square + EPS)
    unit = left_ref[...] / beta
    raw = unit - GAMMA * (total / beta)
    if not first:
        raw = raw - beta * right_ref[...]
    raw_ref[...] = raw
    unit_ref[...] = unit
    norm_ref[...] = jnp.broadcast_to(beta, norm_ref.shape)
    store_message(out_ref, raw, jnp.sum(raw * raw, axis=0, keepdims=True))


def forward_end_kernel(msg_ref, raw_ref, unit_ref, left_ref, right_ref, norm_ref, square_ref, out_ref):
    total, square = summed_messages(msg_ref)
    alpha = jnp.sqrt(square + EPS)
    right = raw_ref[...] / alpha
    left = right - GAMMA * (total / alpha) - alpha * unit_ref[...]
    left_ref[...] = left
    right_ref[...] = right
    norm_ref[...] = jnp.broadcast_to(alpha, norm_ref.shape)
    own = jnp.sum(left * left, axis=0, keepdims=True)
    square_ref[...] = jnp.broadcast_to(own, square_ref.shape)
    store_message(out_ref, left, own)


VMEM = pl.BlockSpec(memory_space=pltpu.VMEM)
SMEM = pl.BlockSpec(memory_space=pltpu.SMEM)
LIMIT = pltpu.CompilerParams(vmem_limit_bytes=32 * 1024 * 1024)


def f32(*shape):
    return jax.ShapeDtypeStruct(shape, F32)


def message(n):
    return jax.ShapeDtypeStruct((n, MSG, CHANS), I16)


def apply_tiles(kernel, name, n_out, vec_tiles, sum_shape, meta, received, own, other):
    return pl.pallas_call(
        kernel,
        out_shape=message(n_out),
        in_specs=[SMEM, VMEM, VMEM, VMEM],
        out_specs=VMEM,
        scratch_shapes=[pltpu.VMEM((vec_tiles, TILE, 2 * CHANS), BF16), pltpu.VMEM(sum_shape, F32)],
        compiler_params=LIMIT,
        cost_estimate=pl.CostEstimate(
            flops=4 * 2 * SLOTS * TILE * TILE * CHANS, bytes_accessed=6 * 1024 * 1024, transcendentals=0
        ),
        name=name,
    )(meta, received, own, other)


def shards(rewards, tile_data, tile_slots, tile_count):
    core = lax.axis_index("core")
    swap = [(0, 1), (1, 0)]

    own = tile_data[0, 0]
    slots = jnp.concatenate([tile_slots[0, 0], tile_count[0, 0][None], jnp.zeros((3,), jnp.int32)])
    sent = lax.dynamic_slice_in_dim(rewards, (1 - core) * CHANS, CHANS, 1)
    kept = lax.dynamic_slice_in_dim(rewards, core * CHANS, CHANS, 1)
    arrived = lax.ppermute(sent, "core", swap)
    rewards_pair = jnp.where(
        core == 0, jnp.concatenate([kept, arrived], axis=0), jnp.concatenate([arrived, kept], axis=0)
    )
    other = lax.ppermute(own, "core", swap)
    other_slots = lax.ppermute(slots, "core", swap)
    meta = jnp.stack([slots, other_slots, jnp.full_like(slots, core)])

    def adjoint(received):
        out = apply_tiles(
            adjoint_kernel, "adjoint", N_ROWS, 4, (TILE_COLS, TILE, CHANS), meta, received, own, other
        )
        return lax.all_to_all(out, ROWS, 0, 0)

    def forward(received):
        out = apply_tiles(
            forward_kernel, "forward", N_COLS, TILE_COLS, (N_COLS, PAIR, CHANS), meta, received, own, other
        )
        return lax.all_to_all(out, COLS, 0, 0)

    def adjoint_end(received, left, right):
        first = right is None
        return pl.pallas_call(
            functools.partial(adjoint_end_kernel, first),
            out_shape=(f32(PAIR, CHANS), f32(PAIR, CHANS), f32(8, CHANS), message(N_ROWS)),
            in_specs=[VMEM] * (2 if first else 3),
            out_specs=(VMEM,) * 4,
            compiler_params=LIMIT,
            name="adjoint_end",
        )(received, left, *(() if first else (right,)))

    def forward_end(received, raw, unit):
        return pl.pallas_call(
            forward_end_kernel,
            out_shape=(f32(PAIR, CHANS), f32(PAIR, CHANS), f32(8, CHANS), f32(8, CHANS), message(N_COLS)),
            in_specs=[VMEM] * 3,
            out_specs=(VMEM,) * 5,
            compiler_params=LIMIT,
            name="forward_end",
        )(received, raw, unit)

    def sum_over_chips(square):
        spread = jnp.broadcast_to(square.reshape(1, 2, 128), (N_ROWS * N_COLS, 2, 128))
        return jnp.sum(lax.all_to_all(spread, ROWS + COLS, 0, 0), axis=0).reshape(CHANS)

    sends = pl.pallas_call(
        first_kernel, out_shape=message(N_COLS), in_specs=[VMEM], out_specs=VMEM, compiler_params=LIMIT, name="first"
    )(rewards_pair)
    raw, unit, beta_rows, sends = adjoint_end(adjoint(lax.all_to_all(sends, COLS, 0, 0)), rewards_pair, None)
    beta_first = beta_rows[0]
    estimate = jnp.zeros_like(rewards_pair)
    phibar = beta_first
    rhobar = None
    direction = None
    theta_rho = None
    sine_val = cosine = None
    for iteration in range(ITERS):
        received = forward(lax.all_to_all(sends, ROWS, 0, 0))
        left, right, alpha_rows, square_rows, sends = forward_end(received, raw, unit)
        alpha_val = alpha_rows[0]
        if iteration == 0:
            rhobar = alpha_val
            direction = right
        else:
            theta_val = sine_val * alpha_val
            rhobar = -cosine * alpha_val
            direction = right - theta_val / rho_val * direction
        if iteration < ITERS - 1:
            raw, unit, beta_rows, sends = adjoint_end(adjoint(lax.all_to_all(sends, COLS, 0, 0)), left, right)
            beta_val = beta_rows[0]
        else:
            beta_val = jnp.sqrt(sum_over_chips(square_rows[0]) + EPS)
            raw, unit, beta_rows, sends = adjoint_end(adjoint(lax.all_to_all(sends, COLS, 0, 0)), left, right)
        rho_val = jnp.sqrt(rhobar * rhobar + beta_val * beta_val)
        cosine = rhobar / rho_val
        sine_val = beta_val / rho_val
        phi_val = cosine * phibar
        phibar = sine_val * phibar
        estimate = estimate + phi_val / rho_val * direction
    residual = phibar / beta_first

    kept = lax.dynamic_slice_in_dim(estimate, core * STATES_DEV, STATES_DEV, 0)
    sent = lax.dynamic_slice_in_dim(estimate, (1 - core) * STATES_DEV, STATES_DEV, 0)
    arrived = lax.ppermute(sent, "core", swap)
    residual_other = lax.ppermute(residual, "core", swap)
    estimate_out = jnp.where(
        core == 0, jnp.concatenate([kept, arrived], axis=1), jnp.concatenate([arrived, kept], axis=1)
    )
    residual_out = jnp.where(
        core == 0, jnp.concatenate([residual, residual_other]), jnp.concatenate([residual_other, residual])
    )
    return (estimate_out, residual_out)


def solution(mesh):
    fine = Mesh(np.asarray(mesh.devices).reshape(SIZES), AXES)
    rows = ("z", "yh", "core")
    return jax.shard_map(
        shards,
        mesh=fine,
        in_specs=(
            P(AXES, None),
            P(rows, COLS, None, None, None),
            P(rows, COLS, None),
            P(rows, COLS),
        ),
        out_specs=(P(AXES, None), P()),
        check_vma=False,
    )
```

time: 1060 us -> 251 us (0.24)
  waiting for transfers between devices: 470 us -> 22 us
  blocking collectives: 443 us -> 178 us
  local copies, waits for them, and re-layouts: 63.1 us -> 1.8 us
  matrix products: 49 us -> 0 us
  Pallas kernels: 0 us -> 24.1 us
  starting transfers between devices: 0.69 us -> 21.6 us
  between operations: 14.9 us -> 1.42 us
  other arithmetic: 14.8 us -> 1.73 us
    psum x5 -> x0, blocking collectives: 397 us -> none  [norm_all(): summed = lax.psum(jnp.sum(values * values, axis=0), ('row', 'col'))]
    reduce_scatter x4 -> x0, waiting for transfers between devices: 317 us -> none  [the longest x2 249 us: adjoint_scatter(): lax.psum_scatter(adjoint_terms(left_vec), 'row', scatter_dimension=0, til...]
    all_to_all x0 -> x7, blocking collectives: none -> 178 us  [the longest x2 77.5 us: adjoint(): return lax.all_to_all(out, ROWS, 0, 0)]
    all_gather x2 -> x0, waiting for transfers between devices: 153 us -> none  [shards(): lax.all_gather(right_vec.astype(jnp.bfloat16), 'row', axis=0, tiled=True)]
    dot_general x8 -> x0, matrix products: 49 us -> none  [the longest x2 13.4 us: backward_part(): jnp.einsum('ts,sjk->tjk', placing, products, precision=lax.Precision.HIGH...]
    all_gather x2 -> x0, blocking collectives: 46.5 us -> none  [adjoint_terms(): lax.all_gather(left_vec.astype(jnp.bfloat16), 'col', axis=0, tiled=True)]
    dot_general x6 -> x0, local copies, waits for them, and re-layouts: 41.1 us -> none  [the longest x2 19.4 us: backward_part(): jnp.einsum('sij,sik->sjk', tile_data, pieces, preferred_element_type=jnp....]
    pallas_call x0 -> x9, Pallas kernels: none -> 24.1 us  [the longest x4 20.3 us: apply_tiles(): pl.pallas_call(kernel, out_shape=message(n_out), in_specs=[SMEM, VMEM, VM...]
  transfers between devices with their start and end apart: 6 -> 7, of which waited for: 6 -> 5; matrix products, arithmetic and copies ran while one was open for 0% -> 1% of each run, Pallas kernels for 0% -> 0%
where the time goes in v1:
time: 251 us; the launch traced here: 250 us
  blocking collectives  178 us (71%)
  Pallas kernels  24.1 us (10%)
  waiting for transfers between devices  22 us (9%)
  starting transfers between devices  21.6 us (9%)
    all_to_all x2, blocking collectives, adjoint(): return lax.all_to_all(out, ROWS, 0, 0)  77.5 us
    all_to_all x2, blocking collectives, shards(): received = forward(lax.all_to_all(sends, ROWS, 0, 0))  66 us
    all_to_all x2, blocking collectives, forward(): return lax.all_to_all(out, COLS, 0, 0)  23.6 us
    pallas_call x4, Pallas kernels, apply_tiles(): pl.pallas_call(kernel, out_shape=message(n_out), in_specs=[SMEM, VMEM, VM...  20.3 us
    all_to_all x1, waiting for transfers between devices, sum_over_chips(): lax.all_to_all(spread, ROWS + COLS, 0, 0)  11 us
    all_to_all x1, blocking collectives, shards(): lax.all_to_all(sends, COLS, 0, 0)  10.5 us
    all_to_all x1, waiting for transfers between devices, shards(): lax.all_to_all(sends, COLS, 0, 0)  7.64 us
    all_to_all x1, starting transfers between devices, sum_over_chips(): lax.all_to_all(spread, ROWS + COLS, 0, 0)  7.64 us
  transfers between devices with their start and end apart: 7, of which 5 were waited for; matrix products, arithmetic and copies ran while one was open for 1% of the time, Pallas kernels for 0%

profile of v1, /device:TPU:1, one launch (start us, length us, event | category | flops | bytes accessed | tf_op | source)
XLA Modules:
  0.0 250.3 jit_solution(3882984027458436732)
XLA Ops:
  0.6 3.3 %collective-permute-start.2 = (bf16[12,256,256]{2,1,0:T(8,128)(2,1)}, bf16[12,256,256]{2,1,0:T(8,128)(2,1)}, u32[]{:S(2)}, u32[]{:S(2)}) collective-permute-start(bf16[12,256,256]{2,1,0:T(8,128)(2,1)} %bitcast.31), channel_id=1, source_target_pairs={{0,8},{8,0},{1,9},{9,1},{2,10},{10,2},{3,11},{11,3},{4,12},{12,4},... | collective-permute-start | bytes 4718600 | tf_op jit(solution)/shard_map/ppermute | solution.py:224
  4.0 1.0 constant_dynamic-slice_fusion.3
  5.0 0.1 collective-permute-start.1
  5.1 2.0 collective-permute-done.1
  7.1 0.9 first.1
  8.0 3.5 %all-to-all-start = ((s16[8,144,256]{2,1,0:T(8,128)(2,1)}), s16[8,144,256]{2,1,0:T(8,128)(2,1)S(1)}, u32[]{:S(2)}, u32[]{:S(2)}) async-start(s16[8,144,256]{2,1,0:T(8,128)(2,1)} %first.1), calls=%async_computation | async-start | bytes 1179648 | tf_op jit(solution)/shard_map/all_to_all | solution.py:268
  12.3 0.4 collective-permute-start
  12.9 0.7 collective-permute-done
  13.6 7.6 %all-to-all-done.msg_ref = s16[8,144,256]{2,1,0:T(8,128)(2,1)S(1)} async-done(((s16[8,144,256]{2,1,0:T(8,128)(2,1)}), s16[8,144,256]{2,1,0:T(8,128)(2,1)S(1)}, u32[]{:S(2)}, u32[]{:S(2)}) %all-to-all-start) | async-done | bytes 589856 | tf_op jit(solution)/shard_map/all_to_all | solution.py:268
  21.3 6.2 %adjoint.2 = s16[16,144,256]{2,1,0:T(8,128)(2,1)S(1)} custom-call(s32[3,16]{1,0:T(4,128)S(1)} %add_add_fusion.meta_ref, s16[8,144,256]{2,1,0:T(8,128)(2,1)S(1)} %all-to-all-done.msg_ref, bf16[12,256,256]{2,1,0:T(8,128)(2,1)S(1)} %bitcast.32, bf16[12,256,256]{2,1,0:T(8,128)(2,1)} %collective-permute-done.2.other_ref), custom_call_target="tpu_custom_call" | custom-call | flops 1610612736 | bytes 6291456 | tf_op jit(solution)/shard_map/adjoint/pallas_call | solution.py:198
  27.5 43.4 %all_to_all.47.msg_ref = s16[16,144,256]{2,1,0:T(8,128)(2,1)S(1)} all-to-all(s16[16,144,256]{2,1,0:T(8,128)(2,1)S(1)} %adjoint.2), channel_id=1, replica_groups=mesh['z'=8,'yh'=2,'core'=2,'x'=4,'yl'=2] {'z','yh'}, dimensions={0} | all-to-all | bytes 2359296 | tf_op jit(solution)/shard_map/all_to_all | solution.py:232
  70.9 0.5 adjoint_end.2
  71.4 33.2 %all_to_all.48.msg_ref = s16[16,144,256]{2,1,0:T(8,128)(2,1)S(1)} all-to-all(s16[16,144,256]{2,1,0:T(8,128)(2,1)S(1)} %get-tuple-element.17), channel_id=1, replica_groups=mesh['z'=8,'yh'=2,'core'=2,'x'=4,'yl'=2] {'z','yh'}, dimensions={0} | all-to-all | bytes 2359296 | tf_op jit(solution)/shard_map/all_to_all | solution.py:277
  104.5 3.9 %forward.2 = s16[8,144,256]{2,1,0:T(8,128)(2,1)S(1)} custom-call(s32[3,16]{1,0:T(4,128)S(1)} %add_add_fusion.meta_ref, s16[16,144,256]{2,1,0:T(8,128)(2,1)S(1)} %all_to_all.48.msg_ref, bf16[12,256,256]{2,1,0:T(8,128)(2,1)S(1)} %bitcast.33, bf16[12,256,256]{2,1,0:T(8,128)(2,1)} %collective-permute-done.2.other_ref), custom_call_target="tpu_custom_call" | custom-call | flops 1610612736 | bytes 6291456 | tf_op jit(solution)/shard_map/forward/pallas_call | solution.py:198
  108.4 12.8 %all_to_all.49.msg_ref = s16[8,144,256]{2,1,0:T(8,128)(2,1)S(1)} all-to-all(s16[8,144,256]{2,1,0:T(8,128)(2,1)S(1)} %forward.2), channel_id=1, replica_groups=mesh['z'=8,'yh'=2,'core'=2,'x'=4,'yl'=2] {'x','yl'}, dimensions={0} | all-to-all | bytes 1179648 | tf_op jit(solution)/shard_map/all_to_all | solution.py:238
  121.2 0.8 forward_end.2
  122.0 10.5 %all_to_all.50.msg_ref = s16[8,144,256]{2,1,0:T(8,128)(2,1)S(1)} all-to-all(s16[8,144,256]{2,1,0:T(8,128)(2,1)S(1)} %get-tuple-element.21), channel_id=1, replica_groups=mesh['z'=8,'yh'=2,'core'=2,'x'=4,'yl'=2] {'x','yl'}, dimensions={0} | all-to-all | bytes 1179648 | tf_op jit(solution)/shard_map/all_to_all | solution.py:288
  132.5 6.3 %adjoint.3 = s16[16,144,256]{2,1,0:T(8,128)(2,1)S(1)} custom-call(s32[3,16]{1,0:T(4,128)S(1)} %add_add_fusion.meta_ref, s16[8,144,256]{2,1,0:T(8,128)(2,1)S(1)} %all_to_all.50.msg_ref, bf16[12,256,256]{2,1,0:T(8,128)(2,1)S(1)} %bitcast.34, bf16[12,256,256]{2,1,0:T(8,128)(2,1)} %collective-permute-done.2.other_ref), custom_call_target="tpu_custom_call" | custom-call | flops 1610612736 | bytes 6291456 | tf_op jit(solution)/shard_map/adjoint/pallas_call | solution.py:198
  138.9 34.0 %all_to_all.51.msg_ref = s16[16,144,256]{2,1,0:T(8,128)(2,1)S(1)} all-to-all(s16[16,144,256]{2,1,0:T(8,128)(2,1)S(1)} %adjoint.3), channel_id=1, replica_groups=mesh['z'=8,'yh'=2,'core'=2,'x'=4,'yl'=2] {'z','yh'}, dimensions={0} | all-to-all | bytes 2359296 | tf_op jit(solution)/shard_map/all_to_all | solution.py:232
  172.9 0.5 adjoint_end.3
  173.4 32.9 %all_to_all.52.msg_ref = s16[16,144,256]{2,1,0:T(8,128)(2,1)S(1)} all-to-all(s16[16,144,256]{2,1,0:T(8,128)(2,1)S(1)} %get-tuple-element.26), channel_id=1, replica_groups=mesh['z'=8,'yh'=2,'core'=2,'x'=4,'yl'=2] {'z','yh'}, dimensions={0} | all-to-all | bytes 2359296 | tf_op jit(solution)/shard_map/all_to_all | solution.py:277
  206.3 3.9 %forward.3 = s16[8,144,256]{2,1,0:T(8,128)(2,1)S(1)} custom-call(s32[3,16]{1,0:T(4,128)S(1)} %add_add_fusion.meta_ref, s16[16,144,256]{2,1,0:T(8,128)(2,1)S(1)} %all_to_all.52.msg_ref, bf16[12,256,256]{2,1,0:T(8,128)(2,1)S(1)} %bitcast.35, bf16[12,256,256]{2,1,0:T(8,128)(2,1)} %collective-permute-done.2.other_ref), custom_call_target="tpu_custom_call" | custom-call | flops 1610612736 | bytes 6291456 | tf_op jit(solution)/shard_map/forward/pallas_call | solution.py:198
  210.2 10.9 %all_to_all.53.msg_ref = s16[8,144,256]{2,1,0:T(8,128)(2,1)S(1)} all-to-all(s16[8,144,256]{2,1,0:T(8,128)(2,1)S(1)} %forward.3), channel_id=1, replica_groups=mesh['z'=8,'yh'=2,'core'=2,'x'=4,'yl'=2] {'x','yl'}, dimensions={0} | all-to-all | bytes 1179648 | tf_op jit(solution)/shard_map/all_to_all | solution.py:238
  221.1 1.1 forward_end.3
  222.2 0.7 broadcast_in_dim.5
  222.8 7.6 %all-to-all-start.8 = ((f32[128,2,128]{2,1,0:T(2,128)}), f32[128,2,128]{2,1,0:T(2,128)S(1)}, u32[]{:S(2)}, u32[]{:S(2)}) async-start(f32[128,2,128]{2,1,0:T(2,128)} %broadcast_in_dim.5), calls=%async_computation.8 | async-start | bytes 262144 | tf_op jit(solution)/shard_map/all_to_all | solution.py:263
  230.5 11.0 %all-to-all-done.8 = f32[128,2,128]{2,1,0:T(2,128)S(1)} async-done(((f32[128,2,128]{2,1,0:T(2,128)}), f32[128,2,128]{2,1,0:T(2,128)S(1)}, u32[]{:S(2)}, u32[]{:S(2)}) %all-to-all-start.8) | async-done | bytes 131104 | tf_op jit(solution)/shard_map/all_to_all | solution.py:263
  241.6 0.1 reduce_sum.9
  241.8 6.4 %collective-permute-start.4 = (f32[256]{0:T(256)S(1)}, f32[256]{0:T(256)S(1)}, u32[]{:S(2)}, u32[]{:S(2)}) collective-permute-start(f32[256]{0:T(256)S(1)} %fusion.3), channel_id=1, source_target_pairs={{0,8},{8,0},{1,9},{9,1},{2,10},{10,2},{3,11},{11,3},{4,12},{12,4},... | collective-permute-start | bytes 3080 | tf_op jit(solution)/shard_map/ppermute | solution.py:304
  248.4 0.7 collective-permute-done.4
  249.0 0.6 maximum_select_fusion.2
  249.6 0.7 maximum_select_fusion.1
  (21 shorter events, 0.6 us)
Async XLA Ops:
  0.6 20.7 %collective-permute-start.2 = (bf16[12,256,256]{2,1,0:T(8,128)(2,1)}, bf16[12,256,256]{2,1,0:T(8,128)(2,1)}, u32[]{:S(2)}, u32[]{:S(2)}) collective-permute-start(bf16[12,256,256]{2,1,0:T(8,128)(2,1)} %bitcast.31), channel_id=1, source_target_pairs={{0,8},{8,0},{1,9},{9,1},{2,10},{10,2},{3,11},{11,3},{4,12},{12,4},... | collective-permute-start | bytes 4718600 | tf_op jit(solution)/shard_map/ppermute | solution.py:224
  4.0 8.3 %copy-start.1 = (s32[1,1,12]{2,1,0:T(1,128)S(1)}, s32[1,1,12]{2,1,0:T(1,128)}, u32[]{:S(2)}) copy-start(s32[1,1,12]{2,1,0:T(1,128)} %param.6) | copy-start | bytes 148
  4.0 17.3 %copy-start = (bf16[1,1,12,256,256]{4,3,2,1,0:T(8,128)(2,1)S(1)}, bf16[1,1,12,256,256]{4,3,2,1,0:T(8,128)(2,1)}, u32[]{:S(2)}) copy-start(bf16[1,1,12,256,256]{4,3,2,1,0:T(8,128)(2,1)} %param.5) | copy-start | bytes 4718596
  5.0 2.1 collective-permute-start.1
  8.0 13.3 %all-to-all-start = ((s16[8,144,256]{2,1,0:T(8,128)(2,1)}), s16[8,144,256]{2,1,0:T(8,128)(2,1)S(1)}, u32[]{:S(2)}, u32[]{:S(2)}) async-start(s16[8,144,256]{2,1,0:T(8,128)(2,1)} %first.1), calls=%async_computation | async-start | bytes 1179648 | tf_op jit(solution)/shard_map/all_to_all | solution.py:268
  12.3 1.3 collective-permute-start
  222.8 18.7 %all-to-all-start.8 = ((f32[128,2,128]{2,1,0:T(2,128)}), f32[128,2,128]{2,1,0:T(2,128)S(1)}, u32[]{:S(2)}, u32[]{:S(2)}) async-start(f32[128,2,128]{2,1,0:T(2,128)} %broadcast_in_dim.5), calls=%async_computation.8 | async-start | bytes 262144 | tf_op jit(solution)/shard_map/all_to_all | solution.py:263
  241.8 7.2 %collective-permute-start.4 = (f32[256]{0:T(256)S(1)}, f32[256]{0:T(256)S(1)}, u32[]{:S(2)}, u32[]{:S(2)}) collective-permute-start(f32[256]{0:T(256)S(1)} %fusion.3), channel_id=1, source_target_pairs={{0,8},{8,0},{1,9},{9,1},{2,10},{10,2},{3,11},{11,3},{4,12},{12,4},... | collective-permute-start | bytes 3080 | tf_op jit(solution)/shard_map/ppermute | solution.py:304
  248.3 1.3 collective-permute-start.3

commit v2 on v1

v2 whole, which is shorter than its diff:
```python
import functools

import jax
import jax.numpy as jnp
import numpy as np
from jax import lax
from jax.experimental import pallas as pl
from jax.experimental.pallas import tpu as pltpu
from jax.sharding import Mesh, PartitionSpec as P

ITERS = 2
EPS = 1e-06
GAMMA = 0.9

AXES = ("z", "yh", "core", "x", "yl")
SIZES = (8, 2, 2, 4, 2)
ROWS = ("z", "yh")
COLS = ("x", "yl")
N_COLS = 8
TILE = 256
STATES_DEV = 64
PAIR = 2 * STATES_DEV
CORE_CHANS = 256
CHANS = 128
BLOCKS = 4
SLOTS = 12
FAR_FIRST = 4
TILE_COLS = 8
HEAD = 16
BITS = 14.0
BF16 = jnp.bfloat16
F32 = jnp.float32
I16 = jnp.int16


def to_i16(values):
    return values.astype(jnp.int32).astype(I16)


def scaled_exponent(largest):
    return jnp.ceil(jnp.log2(jnp.maximum(largest, 1e-30)))


def head_rows(exponent, square):
    square_exp = scaled_exponent(square)
    mantissa = square * jnp.exp2(-square_exp) * 16384.0
    high = jnp.round(mantissa)
    low = jnp.round((mantissa - high) * 16384.0)
    row = lax.broadcasted_iota(jnp.int32, (HEAD, exponent.shape[-1]), 0)
    rows = jnp.where(row == 0, exponent, jnp.where(row == 1, square_exp, jnp.where(row == 2, high, low)))
    return to_i16(rows)


def read_head(head):
    rows = head.astype(jnp.int32).astype(F32)
    step = jnp.exp2(rows[0:1] - BITS)
    square = (rows[2:3] + rows[3:4] * (1.0 / 16384.0)) * (1.0 / 16384.0) * jnp.exp2(rows[1:2])
    return step, square


def quantized(block):
    exponent = scaled_exponent(jnp.max(jnp.abs(block), axis=0, keepdims=True))
    return to_i16(jnp.round(block * jnp.exp2(BITS - exponent))), exponent


def store_message(out_ref, index, block, square):
    values, exponent = quantized(block)
    head = head_rows(exponent, square)
    rows = block.shape[0]
    for i in range(out_ref.shape[0]) if index is None else (index,):
        out_ref[i, :rows, :] = values
        out_ref[i, rows:, :] = head


def wide(values):
    return values.astype(jnp.int32).astype(F32)


def split_store(ref, index, rows, values):
    high = values.astype(BF16)
    chans = values.shape[-1]
    ref[index, rows, :chans] = high
    ref[index, rows, chans:] = (values - high.astype(F32)).astype(BF16)


def tile_at(refs, which, s):
    if which < 2:
        return refs[which][s]
    at = 2 * which - 2
    return refs[at][s] if s < FAR_FIRST else refs[at + 1][s - FAR_FIRST]


def column_of(meta_ref, which, s):
    return jnp.where(s < meta_ref[which, SLOTS], meta_ref[which, s] % TILE_COLS, TILE_COLS)


def forward_kernel(meta_ref, msg_ref, *refs):
    tile_refs, (out_ref, vec_ref, sum_ref) = refs[:-3], refs[-3:]
    square = jnp.zeros((1, CHANS), F32)
    for k in range(TILE_COLS):
        step, part = read_head(msg_ref[k, TILE:, :])
        square = square + part
        split_store(vec_ref, k, slice(None), wide(msg_ref[k, :TILE, :]) * step)
    vec_ref[TILE_COLS] = jnp.zeros((TILE, 2 * CHANS), BF16)
    for which in range(BLOCKS):
        block = meta_ref[BLOCKS, which]
        start = meta_ref[which, 0] // TILE_COLS
        for parity in range(2):
            slots = range(parity, SLOTS, 2)
            row = jnp.concatenate([tile_at(tile_refs, which, s) for s in slots], axis=1)
            vec = jnp.concatenate([vec_ref[column_of(meta_ref, which, s)] for s in slots], axis=0)
            total = jnp.dot(row, vec, preferred_element_type=F32)
            summed = total[:, :CHANS] + total[:, CHANS:]
            tile_row = (start + parity) % 2
            for q in range(4):
                sum_ref[tile_row * 4 + q, pl.ds(block * STATES_DEV, STATES_DEV), :] = summed[
                    q * STATES_DEV : (q + 1) * STATES_DEV
                ]
    for k in range(N_COLS):
        store_message(out_ref, k, sum_ref[k], square)


def adjoint_sums(meta_ref, msg_ref, tile_refs, vec_ref, sum_ref):
    chans = msg_ref.shape[-1]
    blocks = msg_ref.shape[1] // STATES_DEV
    square = jnp.zeros((1, chans), F32)
    for k in range(N_COLS):
        step, part = read_head(msg_ref[k, blocks * STATES_DEV :, :])
        square = square + part
        for block in range(blocks):
            values = wide(msg_ref[k, block * STATES_DEV : (block + 1) * STATES_DEV, :]) * step
            split_store(vec_ref, block * 2 + k // 4, pl.ds((k % 4) * STATES_DEV, STATES_DEV), values)
    sum_ref[...] = jnp.zeros_like(sum_ref)
    for which in range(blocks):
        block = meta_ref[BLOCKS, which] % blocks
        start = meta_ref[which, 0] // TILE_COLS
        for parity in range(2):
            vec = vec_ref[block * 2 + (start + parity) % 2]
            for s in range(parity, SLOTS, 2):
                product = lax.dot_general(
                    tile_at(tile_refs, which, s), vec, (((0,), (0,)), ((), ())), preferred_element_type=F32
                )
                sum_ref[column_of(meta_ref, which, s)] += product[:, :chans] + product[:, chans:]
    return square


def adjoint_kernel(meta_ref, msg_ref, *refs):
    tile_refs, (out_ref, vec_ref, sum_ref) = refs[:-3], refs[-3:]
    square = adjoint_sums(meta_ref, msg_ref, tile_refs, vec_ref, sum_ref)
    for k in range(TILE_COLS):
        store_message(out_ref, k, sum_ref[k], square)


def first_adjoint_kernel(meta_ref, msg_ref, *refs):
    tile_refs, (kept_ref, square_ref, out_ref, vec_ref, sum_ref) = refs[:-5], refs[-5:]
    square = adjoint_sums(meta_ref, msg_ref, tile_refs, vec_ref, sum_ref)
    square_ref[...] = jnp.broadcast_to(square[:, :CHANS], square_ref.shape)
    for k in range(TILE_COLS):
        kept_ref[k] = sum_ref[k, :, :CHANS]
        store_message(out_ref, k, sum_ref[k, :, CHANS:], square[:, CHANS:])


def combine_kernel(kept_ref, square_ref, msg_ref, out_ref):
    for k in range(TILE_COLS):
        step, square = read_head(msg_ref[k, TILE:, :])
        total = kept_ref[k] + wide(msg_ref[k, :TILE, :]) * step
        store_message(out_ref, k, total, square_ref[0:1] + square)


def summed_messages(msg_ref):
    total = jnp.zeros((TILE, CHANS), F32)
    square = jnp.zeros((1, CHANS), F32)
    for k in range(msg_ref.shape[0]):
        step, part = read_head(msg_ref[k, TILE:, :])
        total = total + wide(msg_ref[k, :TILE, :]) * step
        square = square + part
    return total, square


def first_kernel(rewards_ref, out_ref):
    rewards = rewards_ref[...]
    store_message(out_ref, None, rewards, jnp.sum(rewards * rewards, axis=0, keepdims=True))


def adjoint_end_kernel(first, msg_ref, left_ref, *refs):
    right_ref, (raw_ref, unit_ref, norm_ref, out_ref) = (None, refs) if first else (refs[0], refs[1:])
    total, square = summed_messages(msg_ref)
    beta = jnp.sqrt(square + EPS)
    unit = left_ref[...] / beta
    raw = unit - GAMMA * (total / beta)
    if not first:
        raw = raw - beta * right_ref[...]
    raw_ref[...] = raw
    unit_ref[...] = unit
    norm_ref[...] = jnp.broadcast_to(beta, norm_ref.shape)
    store_message(out_ref, None, raw, jnp.sum(raw * raw, axis=0, keepdims=True))


def forward_end_kernel(msg_ref, raw_ref, unit_ref, left_ref, right_ref, norm_ref, out_ref):
    total, square = summed_messages(msg_ref)
    alpha = jnp.sqrt(square + EPS)
    right = raw_ref[...] / alpha
    left = right - GAMMA * (total / alpha) - alpha * unit_ref[...]
    left_ref[...] = left
    right_ref[...] = right
    norm_ref[...] = jnp.broadcast_to(alpha, norm_ref.shape)
    store_message(out_ref, None, left, jnp.sum(left * left, axis=0, keepdims=True))


def last_end_kernel(msg_ref, raw_ref, unit_ref, out_ref):
    total, square = summed_messages(msg_ref)
    alpha = jnp.sqrt(square + EPS)
    left = raw_ref[...] / alpha - GAMMA * (total / alpha) - alpha * unit_ref[...]
    own = jnp.sum(left * left, axis=0, keepdims=True)
    out_ref[...] = jnp.broadcast_to(jnp.concatenate([own, alpha], axis=0)[None], out_ref.shape)


VMEM = pl.BlockSpec(memory_space=pltpu.VMEM)
SMEM = pl.BlockSpec(memory_space=pltpu.SMEM)
LIMIT = pltpu.CompilerParams(vmem_limit_bytes=32 * 1024 * 1024)


def f32(*shape):
    return jax.ShapeDtypeStruct(shape, F32)


def message(n, rows=TILE, chans=CHANS):
    return jax.ShapeDtypeStruct((n, rows + HEAD, chans), I16)


def apply_tiles(kernel, name, outs, vec_tiles, n_sums, chans, meta, received, tiles):
    return pl.pallas_call(
        kernel,
        out_shape=outs,
        in_specs=[SMEM] + [VMEM] * (1 + len(tiles)),
        out_specs=jax.tree.map(lambda _: VMEM, outs),
        scratch_shapes=[
            pltpu.VMEM((vec_tiles + 1, TILE, 2 * chans), BF16),
            pltpu.VMEM((n_sums + 1, TILE, chans), F32),
        ],
        compiler_params=LIMIT,
        cost_estimate=pl.CostEstimate(
            flops=4 * (BLOCKS * CHANS) * SLOTS * TILE * TILE, bytes_accessed=6 * 1024 * 1024, transcendentals=0
        ),
        name=name,
    )(meta, received, *tiles)


def shards(rewards, tile_data, tile_slots, tile_count):
    core, yh = lax.axis_index("core"), lax.axis_index("yh")
    swap = [(0, 1), (1, 0)]

    def in_order(at, kept, arrived, axis):
        return jnp.where(
            at == 0, jnp.concatenate([kept, arrived], axis=axis), jnp.concatenate([arrived, kept], axis=axis)
        )

    def exchange(name, at, values, axis):
        size = values.shape[axis] // 2
        kept = lax.dynamic_slice_in_dim(values, at * size, size, axis)
        return kept, lax.ppermute(lax.dynamic_slice_in_dim(values, (1 - at) * size, size, axis), name, swap)

    own = tile_data[0, 0]
    slots = jnp.concatenate([tile_slots[0, 0], tile_count[0, 0][None], jnp.zeros((3,), jnp.int32)])
    rewards_pair = in_order(core, *exchange("core", core, rewards, 1), 0)
    rewards_kept = lax.dynamic_slice_in_dim(rewards_pair, yh * CHANS, CHANS, 1)
    rewards_sent = lax.dynamic_slice_in_dim(rewards_pair, (1 - yh) * CHANS, CHANS, 1)
    rewards_arrived = lax.ppermute(rewards_sent, "yh", swap)
    pair = [own, lax.ppermute(own, "core", swap)]
    pair_slots = jnp.stack([slots, lax.ppermute(slots, "core", swap)])
    far_slots = lax.ppermute(pair_slots, "yh", swap)
    here, there = yh * 2, (1 - yh) * 2
    places = jnp.stack([here + core, here + 1 - core, there + core, there + 1 - core]).astype(jnp.int32)
    places = jnp.concatenate([places, jnp.zeros((12,), jnp.int32)])[None]

    def first_adjoint(received, own_last):
        pair_meta = jnp.concatenate([pair_slots, pair_slots, places])
        kept, square, sent = apply_tiles(
            first_adjoint_kernel,
            "first_adjoint",
            (f32(TILE_COLS, TILE, CHANS), f32(8, CHANS), message(TILE_COLS)),
            4, TILE_COLS, CORE_CHANS, pair_meta, received, pair,
        )
        arrived = lax.ppermute(sent, "yh", swap)
        own_last, *_ = lax.optimization_barrier((own_last, arrived, rewards_arrived, far_slots))
        far = lax.ppermute(own_last, "yh", swap)
        out = pl.pallas_call(
            combine_kernel,
            out_shape=message(TILE_COLS),
            in_specs=[VMEM] * 3,
            out_specs=VMEM,
            compiler_params=LIMIT,
            name="combine",
        )(kept, square, arrived)
        return out, far

    def adjoint(received):
        out = apply_tiles(
            adjoint_kernel, "adjoint", message(TILE_COLS), 8, TILE_COLS, CHANS, meta, received, tiles
        )
        return lax.all_to_all(out, "z", 0, 0)

    def forward(received):
        out = apply_tiles(forward_kernel, "forward", message(N_COLS), TILE_COLS, N_COLS, CHANS, meta, received, tiles)
        return lax.all_to_all(out, COLS, 0, 0)

    def adjoint_end(received, left, right):
        first = right is None
        return pl.pallas_call(
            functools.partial(adjoint_end_kernel, first),
            out_shape=(f32(TILE, CHANS), f32(TILE, CHANS), f32(8, CHANS), message(TILE_COLS)),
            in_specs=[VMEM] * (2 if first else 3),
            out_specs=(VMEM,) * 4,
            compiler_params=LIMIT,
            name="adjoint_end",
        )(received, left, *(() if first else (right,)))

    def forward_end(received, raw, unit):
        return pl.pallas_call(
            forward_end_kernel,
            out_shape=(f32(TILE, CHANS), f32(TILE, CHANS), f32(8, CHANS), message(N_COLS)),
            in_specs=[VMEM] * 3,
            out_specs=(VMEM,) * 4,
            compiler_params=LIMIT,
            name="forward_end",
        )(received, raw, unit)

    def last_end(received, raw, unit):
        spread = pl.pallas_call(
            last_end_kernel,
            out_shape=f32(128, 2, CHANS),
            in_specs=[VMEM] * 3,
            out_specs=VMEM,
            compiler_params=LIMIT,
            name="last_end",
        )(received, raw, unit)
        parts = lax.all_to_all(spread, ("yh", "z", "x", "yl"), 0, 0).reshape(2, 64, 2, CHANS)
        rows = jnp.stack([jnp.sum(parts[:, :, 0], axis=1), parts[:, 0, 1]]).reshape(2, CORE_CHANS)
        rows = in_order(core, rows, lax.ppermute(rows, "core", swap), 1)
        return rows[0], rows[1]

    def send_home(vectors, scalars):
        n = len(vectors)
        rows = jnp.stack(scalars)
        rows = jnp.concatenate([rows, jnp.zeros((8 - len(scalars), CHANS), F32)])
        size = PAIR
        stacked = jnp.stack(vectors)
        for name, at, last in (("yh", yh, False), ("core", core, True)):
            width = stacked.shape[-1]
            kept = lax.dynamic_slice_in_dim(stacked, at * size, size, 1).reshape(n * size, width)
            sent = lax.dynamic_slice_in_dim(stacked, (1 - at) * size, size, 1).reshape(n * size, width)
            arrived = lax.ppermute(jnp.concatenate([sent, rows]), name, swap)
            both = in_order(at, jnp.concatenate([kept, rows]), arrived, 1)
            stacked, rows = both[:-8].reshape(n, size, 2 * width), both[-8:]
            size //= 2
        return [stacked[i] for i in range(n)], [rows[i] for i in range(len(scalars))]

    sends = pl.pallas_call(
        first_kernel,
        out_shape=message(N_COLS, PAIR, CORE_CHANS),
        in_specs=[VMEM],
        out_specs=VMEM,
        compiler_params=LIMIT,
        name="first",
    )(jnp.concatenate([rewards_kept, rewards_sent], axis=1))
    own_first, _ = lax.optimization_barrier((own[:FAR_FIRST], sends))
    far_first = lax.ppermute(own_first, "yh", swap)
    received = lax.all_to_all(sends, COLS, 0, 0)
    meta = jnp.concatenate([pair_slots, far_slots, places])
    rewards_own = in_order(yh, rewards_kept, rewards_arrived, 0)
    sends, far_last = first_adjoint(received, own[FAR_FIRST:])
    raw, unit, beta_rows, sends = adjoint_end(lax.all_to_all(sends, "z", 0, 0), rewards_own, None)
    far_last, _ = lax.optimization_barrier((far_last, sends))
    far = [far_first, far_last]
    tiles = pair + far + [lax.ppermute(part, "core", swap) for part in far]
    raws, alphas, betas = [raw], [], [beta_rows[0]]
    for iteration in range(ITERS):
        received = forward(lax.all_to_all(sends, "z", 0, 0))
        if iteration == ITERS - 1:
            raws, scalars = send_home(raws, betas + alphas)
            next_square, last_alpha = last_end(received, raw, unit)
        left, right, alpha_rows, sends = forward_end(received, raw, unit)
        raw, unit, beta_rows, sends = adjoint_end(adjoint(lax.all_to_all(sends, COLS, 0, 0)), left, right)
        if iteration < ITERS - 1:
            raws.append(raw)
            alphas.append(alpha_rows[0])
            betas.append(beta_rows[0])
    betas, alphas = scalars[:ITERS] + [jnp.sqrt(next_square + EPS)], scalars[ITERS:] + [last_alpha]

    phibar, rhobar = betas[0], alphas[0]
    direction = [1.0 / alphas[0]]
    estimate = []
    for iteration in range(ITERS):
        beta_val = betas[iteration + 1]
        rho_val = jnp.sqrt(rhobar * rhobar + beta_val * beta_val)
        cosine = rhobar / rho_val
        sine_val = beta_val / rho_val
        phi_val = cosine * phibar
        phibar = sine_val * phibar
        weight = phi_val / rho_val
        estimate = [e + weight * d for e, d in zip(estimate + [0.0], direction)]
        if iteration < ITERS - 1:
            alpha_val = alphas[iteration + 1]
            theta_val = sine_val * alpha_val
            rhobar = -cosine * alpha_val
            direction = [-(theta_val / rho_val) * d for d in direction] + [1.0 / alpha_val]
    total = sum(e[None, :] * w for e, w in zip(estimate, raws))
    return (total, phibar / betas[0])


def solution(mesh):
    fine = Mesh(np.asarray(mesh.devices).reshape(SIZES), AXES)
    rows = ("z", "yh", "core")
    return jax.shard_map(
        shards,
        mesh=fine,
        in_specs=(
            P(AXES, None),
            P(rows, COLS, None, None, None),
            P(rows, COLS, None),
            P(rows, COLS),
        ),
        out_specs=(P(AXES, None), P()),
        check_vma=False,
    )
```

time: 251 us -> 213 us (0.85)
  blocking collectives: 178 us -> 58 us
  waiting for transfers between devices: 22 us -> 62.2 us
  starting transfers between devices: 21.6 us -> 60.3 us
  local copies, waits for them, and re-layouts: 1.8 us -> 8.12 us
  Pallas kernels: 24.1 us -> 19 us
    all_to_all x4 -> x2, blocking collectives: 144 us -> 33.5 us  [the longest x1 17.1 us: adjoint(): return lax.all_to_all(out, 'z', 0, 0)]
    all_to_all x2 -> x5, waiting for transfers between devices: 18.7 us -> 47.5 us  [the longest x1 14.9 us: shards(): received = forward(lax.all_to_all(sends, 'z', 0, 0))]
    ppermute x5 -> x13, starting transfers between devices: 10.4 us -> 30.2 us  [the longest x2 8.09 us: send_home(): arrived = lax.ppermute(jnp.concatenate([sent, rows]), name, swap)]
    all_to_all x2 -> x5, starting transfers between devices: 11.2 us -> 30.1 us  [the longest x1 9.15 us: last_end(): lax.all_to_all(spread, ('yh', 'z', 'x', 'yl'), 0, 0)]
    ppermute x5 -> x13, waiting for transfers between devices: 3.32 us -> 14.7 us  [the longest x1 8.74 us: shards(): far_slots = lax.ppermute(pair_slots, 'yh', swap)]
    all_to_all x2 -> x1, blocking collectives: 23.6 us -> 13 us  [forward(): return lax.all_to_all(out, COLS, 0, 0)]
    pallas_call x7 -> x8, Pallas kernels: 23.2 us -> 17.3 us  [the longest x4 15.7 us: apply_tiles(): pl.pallas_call(kernel, out_shape=outs, in_specs=[SMEM] + [VMEM] * (1 + le...]
    unnamed x4 -> x22, local copies, waits for them, and re-layouts: 0.01 us -> 5.11 us
  transfers between devices with their start and end apart: 7 -> 18, of which waited for: 5 -> 11; matrix products, arithmetic and copies ran while one was open for 1% -> 2% of each run, Pallas kernels for 0% -> 1%
where the time goes in v2:
time: 213 us; the launch traced here: 212 us
  waiting for transfers between devices  62.2 us (29%)
  starting transfers between devices  60.3 us (28%)
  blocking collectives  58 us (27%)
  Pallas kernels  19 us (9%)
  local copies, waits for them, and re-layouts  8.12 us (4%)
  other arithmetic  2.44 us (1%)
    all_to_all x1, blocking collectives, adjoint(): return lax.all_to_all(out, 'z', 0, 0)  17.1 us
    all_to_all x1, blocking collectives, shards(): received = forward(lax.all_to_all(sends, 'z', 0, 0))  16.4 us
    pallas_call x4, Pallas kernels, apply_tiles(): pl.pallas_call(kernel, out_shape=outs, in_specs=[SMEM] + [VMEM] * (1 + le...  15.7 us
    all_to_all x1, waiting for transfers between devices, shards(): received = forward(lax.all_to_all(sends, 'z', 0, 0))  14.9 us
    all_to_all x1, waiting for transfers between devices, shards(): lax.all_to_all(sends, 'z', 0, 0)  14.4 us
    all_to_all x1, blocking collectives, forward(): return lax.all_to_all(out, COLS, 0, 0)  13 us
    all_to_all x1, blocking collectives, shards(): lax.all_to_all(sends, COLS, 0, 0)  11.4 us
    all_to_all x1, starting transfers between devices, last_end(): lax.all_to_all(spread, ('yh', 'z', 'x', 'yl'), 0, 0)  9.15 us
  transfers between devices with their start and end apart: 18, of which 11 were waited for; matrix products, arithmetic and copies ran while one was open for 2% of the time, Pallas kernels for 1%

profile of v2, /device:TPU:1, one launch (start us, length us, event | category | flops | bytes accessed | tf_op | source)
XLA Modules:
  0.0 211.6 jit_solution(13717965946032913676)
XLA Ops:
  0.7 3.3 %collective-permute-start.2 = (bf16[12,256,256]{2,1,0:T(8,128)(2,1)}, bf16[12,256,256]{2,1,0:T(8,128)(2,1)S(1)}, u32[]{:S(2)}, u32[]{:S(2)}) collective-permute-start(bf16[12,256,256]{2,1,0:T(8,128)(2,1)} %bitcast.35), channel_id=1, source_target_pairs={{0,8},{8,0},{1,9},{9,1},{2,10},{10,2},{3,11},{11,3},{4,12},{12,4},... | collective-permute-start | bytes 4718600 | tf_op jit(solution)/shard_map/ppermute | solution.py:269
  5.1 2.0 collective-permute-done.1
  8.1 4.2 %all-to-all-start = ((s16[8,144,256]{2,1,0:T(8,128)(2,1)}), s16[8,144,256]{2,1,0:T(8,128)(2,1)}, u32[]{:S(2)}, u32[]{:S(2)}) async-start(s16[8,144,256]{2,1,0:T(8,128)(2,1)} %copy-done.4), calls=%async_computation | async-start | bytes 1179648 | tf_op jit(solution)/shard_map/all_to_all | solution.py:368
  14.3 7.9 %all-to-all-done.msg_ref = s16[8,144,256]{2,1,0:T(8,128)(2,1)} async-done(((s16[8,144,256]{2,1,0:T(8,128)(2,1)}), s16[8,144,256]{2,1,0:T(8,128)(2,1)}, u32[]{:S(2)}, u32[]{:S(2)}) %all-to-all-start) | async-done | bytes 589856 | tf_op jit(solution)/shard_map/all_to_all | solution.py:368
  22.2 3.6 %first_adjoint.1 = (f32[8,256,128]{2,1,0:T(8,128)S(1)}, f32[8,128]{1,0:T(8,128)S(1)}, s16[8,272,128]{2,1,0:T(8,128)(2,1)S(1)}) custom-call(s32[5,16]{1,0:T(8,128)S(1)} %concatenate.65.meta_ref, s16[8,144,256]{2,1,0:T(8,128)(2,1)} %all-to-all-done.msg_ref, bf16[12,256,256]{2,1,0:T(8,128)(2,1)S(1)} %bitcast.36, ...), custom_call_target="tpu_custom_call" | custom-call | flops 1610612736 | bytes 6291456 | tf_op jit(solution)/shard_map/first_adjoint/pallas_call | solution.py:232
  25.9 1.8 collective-permute-start.3
  27.6 1.3 collective-permute-start.5
  28.9 1.7 collective-permute-start.4
  31.6 8.7 %collective-permute-done.5 = s32[2,16]{1,0:T(2,128)S(1)} collective-permute-done((s32[2,16]{1,0:T(2,128)S(1)}, s32[2,16]{1,0:T(2,128)S(1)}, u32[]{:S(2)}, u32[]{:S(2)}) %collective-permute-start.5) | collective-permute-done | bytes 160 | tf_op jit(solution)/shard_map/ppermute | solution.py:271
  40.4 1.4 collective-permute-done.4
  41.8 1.5 collective-permute-start.7
  44.5 8.2 %all-to-all-start.1 = ((s16[8,272,128]{2,1,0:T(8,128)(2,1)}), s16[8,272,128]{2,1,0:T(8,128)(2,1)}, u32[]{:S(2)}, u32[]{:S(2)}) async-start(s16[8,272,128]{2,1,0:T(8,128)(2,1)} %copy-done.6), calls=%async_computation.1 | async-start | bytes 1114112 | tf_op jit(solution)/shard_map/all_to_all | solution.py:372
  53.9 14.4 %all-to-all-done.1.msg_ref = s16[8,272,128]{2,1,0:T(8,128)(2,1)} async-done(((s16[8,272,128]{2,1,0:T(8,128)(2,1)}), s16[8,272,128]{2,1,0:T(8,128)(2,1)}, u32[]{:S(2)}, u32[]{:S(2)}) %all-to-all-start.1) | async-done | bytes 557088 | tf_op jit(solution)/shard_map/all_to_all | solution.py:372
  68.2 1.3 adjoint_end.2
  70.4 3.7 %collective-permute-start.9 = (bf16[8,256,256]{2,1,0:T(8,128)(2,1)}, bf16[8,256,256]{2,1,0:T(8,128)(2,1)}, u32[]{:S(2)}, u32[]{:S(2)}) collective-permute-start(bf16[8,256,256]{2,1,0:T(8,128)(2,1)} %collective-permute-done.7.refs_3_), channel_id=1, source_target_pairs={{0,8},{8,0},{1,9},{9,1},{2,10},{10,2},{3,11},{11,3},{4,12},{12,4},... | collective-permute-start | bytes 3145736 | tf_op jit(solution)/shard_map/ppermute | solution.py:375
  74.1 5.0 %all-to-all-start.2 = ((s16[8,272,128]{2,1,0:T(8,128)(2,1)}), s16[8,272,128]{2,1,0:T(8,128)(2,1)}, u32[]{:S(2)}, u32[]{:S(2)}) async-start(s16[8,272,128]{2,1,0:T(8,128)(2,1)} %copy-done.7), calls=%async_computation.2 | async-start | bytes 1114112 | tf_op jit(solution)/shard_map/all_to_all | solution.py:378
  79.1 1.3 collective-permute-start.8
  83.0 14.9 %all-to-all-done.2.msg_ref = s16[8,272,128]{2,1,0:T(8,128)(2,1)} async-done(((s16[8,272,128]{2,1,0:T(8,128)(2,1)}), s16[8,272,128]{2,1,0:T(8,128)(2,1)}, u32[]{:S(2)}, u32[]{:S(2)}) %all-to-all-start.2) | async-done | bytes 557088 | tf_op jit(solution)/shard_map/all_to_all | solution.py:378
  99.0 4.1 %forward.2 = s16[8,272,128]{2,1,0:T(8,128)(2,1)S(1)} custom-call(s32[5,16]{1,0:T(8,128)S(1)} %pad_add_fusion.meta_ref, s16[8,272,128]{2,1,0:T(8,128)(2,1)} %all-to-all-done.2.msg_ref, bf16[12,256,256]{2,1,0:T(8,128)(2,1)S(1)} %bitcast.37, bf16[12,256,256]{2,1,0:T(8,128)(2,1)S(1)} %collective-permute-done.2.refs_1_, ...), custom_call_target="tpu_custom_call" | custom-call | flops 1610612736 | bytes 6291456 | tf_op jit(solution)/shard_map/forward/pallas_call | solution.py:232
  103.1 13.0 %all_to_all.47.msg_ref = s16[8,272,128]{2,1,0:T(8,128)(2,1)S(1)} all-to-all(s16[8,272,128]{2,1,0:T(8,128)(2,1)S(1)} %forward.2), channel_id=1, replica_groups=mesh['z'=8,'yh'=2,'core'=2,'x'=4,'yl'=2] {'x','yl'}, dimensions={0} | all-to-all | bytes 1114112 | tf_op jit(solution)/shard_map/all_to_all | solution.py:305
  116.5 11.4 %all_to_all.48.msg_ref = s16[8,272,128]{2,1,0:T(8,128)(2,1)S(1)} all-to-all(s16[8,272,128]{2,1,0:T(8,128)(2,1)S(1)} %get-tuple-element.29), channel_id=1, replica_groups=mesh['z'=8,'yh'=2,'core'=2,'x'=4,'yl'=2] {'x','yl'}, dimensions={0} | all-to-all | bytes 1114112 | tf_op jit(solution)/shard_map/all_to_all | solution.py:383
  127.9 4.0 %adjoint.1 = s16[8,272,128]{2,1,0:T(8,128)(2,1)S(1)} custom-call(s32[5,16]{1,0:T(8,128)S(1)} %pad_add_fusion.meta_ref, s16[8,272,128]{2,1,0:T(8,128)(2,1)S(1)} %all_to_all.48.msg_ref, bf16[12,256,256]{2,1,0:T(8,128)(2,1)S(1)} %bitcast.38, bf16[12,256,256]{2,1,0:T(8,128)(2,1)S(1)} %collective-permute-done.2.refs_1_, ...), custom_call_target="tpu_custom_call" | custom-call | flops 1610612736 | bytes 6291456 | tf_op jit(solution)/shard_map/adjoint/pallas_call | solution.py:232
  131.9 17.1 %all_to_all.49.msg_ref = s16[8,272,128]{2,1,0:T(8,128)(2,1)S(1)} all-to-all(s16[8,272,128]{2,1,0:T(8,128)(2,1)S(1)} %adjoint.1), channel_id=1, replica_groups=mesh['z'=8,'yh'=2,'core'=2,'x'=4,'yl'=2] {'z'}, dimensions={0} | all-to-all | bytes 1114112 | tf_op jit(solution)/shard_map/all_to_all | solution.py:301
  149.3 16.4 %all_to_all.50.msg_ref = s16[8,272,128]{2,1,0:T(8,128)(2,1)S(1)} all-to-all(s16[8,272,128]{2,1,0:T(8,128)(2,1)S(1)} %get-tuple-element.36), channel_id=1, replica_groups=mesh['z'=8,'yh'=2,'core'=2,'x'=4,'yl'=2] {'z'}, dimensions={0} | all-to-all | bytes 1114112 | tf_op jit(solution)/shard_map/all_to_all | solution.py:378
  165.7 4.0 %forward.3 = s16[8,272,128]{2,1,0:T(8,128)(2,1)S(1)} custom-call(s32[5,16]{1,0:T(8,128)S(1)} %pad_add_fusion.meta_ref, s16[8,272,128]{2,1,0:T(8,128)(2,1)S(1)} %all_to_all.50.msg_ref, bf16[12,256,256]{2,1,0:T(8,128)(2,1)S(1)} %bitcast.39, bf16[12,256,256]{2,1,0:T(8,128)(2,1)S(1)} %collective-permute-done.2.refs_1_, ...), custom_call_target="tpu_custom_call" | custom-call | flops 1610612736 | bytes 6291456 | tf_op jit(solution)/shard_map/forward/pallas_call | solution.py:232
  170.5 3.5 %all-to-all-start.7 = ((s16[8,272,128]{2,1,0:T(8,128)(2,1)}), s16[8,272,128]{2,1,0:T(8,128)(2,1)S(1)}, u32[]{:S(2)}, u32[]{:S(2)}) async-start(s16[8,272,128]{2,1,0:T(8,128)(2,1)} %copy-done.5), calls=%async_computation.7 | async-start | bytes 1114112 | tf_op jit(solution)/shard_map/all_to_all | solution.py:305
  174.2 2.7 %collective-permute-start.10 = (f32[264,128]{1,0:T(8,128)S(1)}, f32[264,128]{1,0:T(8,128)S(1)}, u32[]{:S(2)}, u32[]{:S(2)}) collective-permute-start(f32[264,128]{1,0:T(8,128)S(1)} %concatenate.73), channel_id=1, source_target_pairs={{0,16},{16,0},{1,17},{17,1},{2,18},{18,2},{3,19},{19,3},{4,20},{20... | collective-permute-start | bytes 405512 | tf_op jit(solution)/shard_map/ppermute | solution.py:352
  176.9 4.4 %all-to-all-done.7.msg_ref = s16[8,272,128]{2,1,0:T(8,128)(2,1)S(1)} async-done(((s16[8,272,128]{2,1,0:T(8,128)(2,1)}), s16[8,272,128]{2,1,0:T(8,128)(2,1)S(1)}, u32[]{:S(2)}, u32[]{:S(2)}) %all-to-all-start.7) | async-done | bytes 557088 | tf_op jit(solution)/shard_map/all_to_all | solution.py:305
  182.2 9.2 %all-to-all-start.8 = ((f32[128,2,128]{2,1,0:T(2,128)}), f32[128,2,128]{2,1,0:T(2,128)S(1)}, u32[]{:S(2)}, u32[]{:S(2)}) async-start(f32[128,2,128]{2,1,0:T(2,128)} %last_end.1), calls=%async_computation.8 | async-start | bytes 262144 | tf_op jit(solution)/shard_map/all_to_all | solution.py:337
  191.5 5.4 %collective-permute-start.11 = (f32[136,256]{1,0:T(8,128)S(1)}, f32[136,256]{1,0:T(8,128)S(1)}, u32[]{:S(2)}, u32[]{:S(2)}) collective-permute-start(f32[136,256]{1,0:T(8,128)S(1)} %pad_maximum_fusion), channel_id=1, source_target_pairs={{0,8},{8,0},{1,9},{9,1},{2,10},{10,2},{3,11},{11,3},{4,12},{12,4},... | collective-permute-start | bytes 417800 | tf_op jit(solution)/shard_map/ppermute | solution.py:352
  196.9 5.9 %all-to-all-done.8 = f32[128,2,128]{2,1,0:T(2,128)S(1)} async-done(((f32[128,2,128]{2,1,0:T(2,128)}), f32[128,2,128]{2,1,0:T(2,128)S(1)}, u32[]{:S(2)}, u32[]{:S(2)}) %all-to-all-start.8) | async-done | bytes 131104 | tf_op jit(solution)/shard_map/all_to_all | solution.py:337
  202.9 6.5 %collective-permute-start.12 = (f32[2,256]{1,0:T(2,128)S(1)}, f32[2,256]{1,0:T(2,128)S(1)}, u32[]{:S(2)}, u32[]{:S(2)}) collective-permute-start(f32[2,256]{1,0:T(2,128)S(1)} %pad_maximum_fusion.2), channel_id=1, source_target_pairs={{0,8},{8,0},{1,9},{9,1},{2,10},{10,2},{3,11},{11,3},{4,12},{12,4},... | collective-permute-start | bytes 6152 | tf_op jit(solution)/shard_map/ppermute | solution.py:339
  (76 shorter events, 15.9 us)
Async XLA Ops:
  0.6 21.6 %copy-start = (bf16[1,1,12,256,256]{4,3,2,1,0:T(8,128)(2,1)S(1)}, bf16[1,1,12,256,256]{4,3,2,1,0:T(8,128)(2,1)}, u32[]{:S(2)}) copy-start(bf16[1,1,12,256,256]{4,3,2,1,0:T(8,128)(2,1)} %param.5) | copy-start | bytes 4718596
  0.6 12.3 %copy-start.9 = (s32[1,1,12]{2,1,0:T(1,128)S(1)}, s32[1,1,12]{2,1,0:T(1,128)}, u32[]{:S(2)}) copy-start(s32[1,1,12]{2,1,0:T(1,128)} %param.6) | copy-start | bytes 148
  0.7 21.6 %collective-permute-start.2 = (bf16[12,256,256]{2,1,0:T(8,128)(2,1)}, bf16[12,256,256]{2,1,0:T(8,128)(2,1)S(1)}, u32[]{:S(2)}, u32[]{:S(2)}) collective-permute-start(bf16[12,256,256]{2,1,0:T(8,128)(2,1)} %bitcast.35), channel_id=1, source_target_pairs={{0,8},{8,0},{1,9},{9,1},{2,10},{10,2},{3,11},{11,3},{4,12},{12,4},... | collective-permute-start | bytes 4718600 | tf_op jit(solution)/shard_map/ppermute | solution.py:269
  4.9 2.2 %collective-permute-start.1 = (f32[64,256]{1,0:T(8,128)S(1)}, f32[64,256]{1,0:T(8,128)S(1)}, u32[]{:S(2)}, u32[]{:S(2)}) collective-permute-start(f32[64,256]{1,0:T(8,128)S(1)} %get-tuple-element.50), channel_id=1, source_target_pairs={{0,8},{8,0},{1,9},{9,1},{2,10},{10,2},{3,11},{11,3},{4,12},{12,4},... | collective-permute-start | bytes 196616 | tf_op jit(solution)/shard_map/ppermute | solution.py:261
  7.3 0.8 copy-start.4
  8.1 14.1 %all-to-all-start = ((s16[8,144,256]{2,1,0:T(8,128)(2,1)}), s16[8,144,256]{2,1,0:T(8,128)(2,1)}, u32[]{:S(2)}, u32[]{:S(2)}) async-start(s16[8,144,256]{2,1,0:T(8,128)(2,1)} %copy-done.4), calls=%async_computation | async-start | bytes 1179648 | tf_op jit(solution)/shard_map/all_to_all | solution.py:368
  13.1 1.2 collective-permute-start
  13.6 12.2 %copy-start.8 = (s32[16]{0:T(128)}, s32[16]{0:T(128)S(1)}, u32[]{:S(2)}) copy-start(s32[16]{0:T(128)S(1)} %concatenate.64) | copy-start | bytes 196
  25.9 15.9 %collective-permute-start.3 = (s16[8,272,128]{2,1,0:T(8,128)(2,1)S(1)}, s16[8,272,128]{2,1,0:T(8,128)(2,1)S(1)}, u32[]{:S(2)}, u32[]{:S(2)}) collective-permute-start(s16[8,272,128]{2,1,0:T(8,128)(2,1)S(1)} %get-tuple-element.22), channel_id=1, source_target_pairs={{0,16},{16,0},{1,17},{17,1},{2,18},{18,2},{3,19},{19,3},{4,20},{20... | collective-permute-start | bytes 1671176 | tf_op jit(solution)/shard_map/ppermute | solution.py:284
  27.6 12.8 %collective-permute-start.5 = (s32[2,16]{1,0:T(2,128)S(1)}, s32[2,16]{1,0:T(2,128)S(1)}, u32[]{:S(2)}, u32[]{:S(2)}) collective-permute-start(s32[2,16]{1,0:T(2,128)S(1)} %pad_add_fusion.1), channel_id=1, source_target_pairs={{0,16},{16,0},{1,17},{17,1},{2,18},{18,2},{3,19},{19,3},{4,20},{20... | collective-permute-start | bytes 392 | tf_op jit(solution)/shard_map/ppermute | solution.py:271
  28.9 12.9 %collective-permute-start.4 = (f32[128,128]{1,0:T(8,128)S(1)}, f32[128,128]{1,0:T(8,128)S(1)}, u32[]{:S(2)}, u32[]{:S(2)}) collective-permute-start(f32[128,128]{1,0:T(8,128)S(1)} %get-tuple-element.48), channel_id=1, source_target_pairs={{0,16},{16,0},{1,17},{17,1},{2,18},{18,2},{3,19},{19,3},{4,20},{20... | collective-permute-start | bytes 196616 | tf_op jit(solution)/shard_map/ppermute | solution.py:268
  40.4 4.1 %copy-start.10 = (s32[2,16]{1,0:T(2,128)}, s32[2,16]{1,0:T(2,128)S(1)}, u32[]{:S(2)}) copy-start(s32[2,16]{1,0:T(2,128)S(1)} %collective-permute-done.5) | copy-start | bytes 388
  41.8 28.6 %collective-permute-start.7 = (bf16[8,256,256]{2,1,0:T(8,128)(2,1)}, bf16[8,256,256]{2,1,0:T(8,128)(2,1)}, u32[]{:S(2)}, u32[]{:S(2)}) collective-permute-start(bf16[8,256,256]{2,1,0:T(8,128)(2,1)} %slice_bitcast_fusion), channel_id=1, source_target_pairs={{0,16},{16,0},{1,17},{17,1},{2,18},{18,2},{3,19},{19,3},{4,20},{20... | collective-permute-start | bytes 3145736 | tf_op jit(solution)/shard_map/ppermute | solution.py:286
  43.7 0.8 copy-start.6
  44.5 23.7 %all-to-all-start.1 = ((s16[8,272,128]{2,1,0:T(8,128)(2,1)}), s16[8,272,128]{2,1,0:T(8,128)(2,1)}, u32[]{:S(2)}, u32[]{:S(2)}) async-start(s16[8,272,128]{2,1,0:T(8,128)(2,1)} %copy-done.6), calls=%async_computation.1 | async-start | bytes 1114112 | tf_op jit(solution)/shard_map/all_to_all | solution.py:372
  53.5 25.6 %collective-permute-start.6 = (bf16[4,256,256]{2,1,0:T(8,128)(2,1)}, bf16[4,256,256]{2,1,0:T(8,128)(2,1)}, u32[]{:S(2)}, u32[]{:S(2)}) collective-permute-start(bf16[4,256,256]{2,1,0:T(8,128)(2,1)} %slice_bitcast_fusion.1), channel_id=1, source_target_pairs={{0,16},{16,0},{1,17},{17,1},{2,18},{18,2},{3,19},{19,3},{4,20},{20... | collective-permute-start | bytes 1572872 | tf_op jit(solution)/shard_map/ppermute | solution.py:367
  69.6 0.8 copy-start.7
  70.4 27.5 %collective-permute-start.9 = (bf16[8,256,256]{2,1,0:T(8,128)(2,1)}, bf16[8,256,256]{2,1,0:T(8,128)(2,1)}, u32[]{:S(2)}, u32[]{:S(2)}) collective-permute-start(bf16[8,256,256]{2,1,0:T(8,128)(2,1)} %collective-permute-done.7.refs_3_), channel_id=1, source_target_pairs={{0,8},{8,0},{1,9},{9,1},{2,10},{10,2},{3,11},{11,3},{4,12},{12,4},... | collective-permute-start | bytes 3145736 | tf_op jit(solution)/shard_map/ppermute | solution.py:375
  74.1 23.8 %all-to-all-start.2 = ((s16[8,272,128]{2,1,0:T(8,128)(2,1)}), s16[8,272,128]{2,1,0:T(8,128)(2,1)}, u32[]{:S(2)}, u32[]{:S(2)}) async-start(s16[8,272,128]{2,1,0:T(8,128)(2,1)} %copy-done.7), calls=%async_computation.2 | async-start | bytes 1114112 | tf_op jit(solution)/shard_map/all_to_all | solution.py:378
  79.1 3.1 %collective-permute-start.8 = (bf16[4,256,256]{2,1,0:T(8,128)(2,1)}, bf16[4,256,256]{2,1,0:T(8,128)(2,1)S(1)}, u32[]{:S(2)}, u32[]{:S(2)}) collective-permute-start(bf16[4,256,256]{2,1,0:T(8,128)(2,1)} %collective-permute-done.6.refs_2_), channel_id=1, source_target_pairs={{0,8},{8,0},{1,9},{9,1},{2,10},{10,2},{3,11},{11,3},{4,12},{12,4},... | collective-permute-start | bytes 1572872 | tf_op jit(solution)/shard_map/ppermute | solution.py:375
  82.2 0.8 copy-start.1
  97.9 1.0 copy-start.2
  103.1 24.8 %copy-start.3 = (bf16[4,256,256]{2,1,0:T(8,128)(2,1)S(1)}, bf16[4,256,256]{2,1,0:T(8,128)(2,1)}, u32[]{:S(2)}) copy-start(bf16[4,256,256]{2,1,0:T(8,128)(2,1)} %copy-done.1) | copy-start | bytes 1572868
  169.7 0.8 copy-start.5
  170.5 10.8 %all-to-all-start.7 = ((s16[8,272,128]{2,1,0:T(8,128)(2,1)}), s16[8,272,128]{2,1,0:T(8,128)(2,1)S(1)}, u32[]{:S(2)}, u32[]{:S(2)}) async-start(s16[8,272,128]{2,1,0:T(8,128)(2,1)} %copy-done.5), calls=%async_computation.7 | async-start | bytes 1114112 | tf_op jit(solution)/shard_map/all_to_all | solution.py:305
  174.2 17.2 %collective-permute-start.10 = (f32[264,128]{1,0:T(8,128)S(1)}, f32[264,128]{1,0:T(8,128)S(1)}, u32[]{:S(2)}, u32[]{:S(2)}) collective-permute-start(f32[264,128]{1,0:T(8,128)S(1)} %concatenate.73), channel_id=1, source_target_pairs={{0,16},{16,0},{1,17},{17,1},{2,18},{18,2},{3,19},{19,3},{4,20},{20... | collective-permute-start | bytes 405512 | tf_op jit(solution)/shard_map/ppermute | solution.py:352
  182.2 20.6 %all-to-all-start.8 = ((f32[128,2,128]{2,1,0:T(2,128)}), f32[128,2,128]{2,1,0:T(2,128)S(1)}, u32[]{:S(2)}, u32[]{:S(2)}) async-start(f32[128,2,128]{2,1,0:T(2,128)} %last_end.1), calls=%async_computation.8 | async-start | bytes 262144 | tf_op jit(solution)/shard_map/all_to_all | solution.py:337
  191.5 17.9 %collective-permute-start.11 = (f32[136,256]{1,0:T(8,128)S(1)}, f32[136,256]{1,0:T(8,128)S(1)}, u32[]{:S(2)}, u32[]{:S(2)}) collective-permute-start(f32[136,256]{1,0:T(8,128)S(1)} %pad_maximum_fusion), channel_id=1, source_target_pairs={{0,8},{8,0},{1,9},{9,1},{2,10},{10,2},{3,11},{11,3},{4,12},{12,4},... | collective-permute-start | bytes 417800 | tf_op jit(solution)/shard_map/ppermute | solution.py:352
  202.9 7.4 %collective-permute-start.12 = (f32[2,256]{1,0:T(2,128)S(1)}, f32[2,256]{1,0:T(2,128)S(1)}, u32[]{:S(2)}, u32[]{:S(2)}) collective-permute-start(f32[2,256]{1,0:T(2,128)S(1)} %pad_maximum_fusion.2), channel_id=1, source_target_pairs={{0,8},{8,0},{1,9},{9,1},{2,10},{10,2},{3,11},{11,3},{4,12},{12,4},... | collective-permute-start | bytes 6152 | tf_op jit(solution)/shard_map/ppermute | solution.py:339

commit v3 on v2

--- a/solution.py
+++ b/solution.py
@@ -24,7 +24,7 @@
 CHANS = 128
 BLOCKS = 4
 SLOTS = 12
-FAR_FIRST = 4
+PART = 6
 TILE_COLS = 8
 HEAD = 16
 BITS = 14.0
@@ -84,10 +84,7 @@
 
 
 def tile_at(refs, which, s):
-    if which < 2:
-        return refs[which][s]
-    at = 2 * which - 2
-    return refs[at][s] if s < FAR_FIRST else refs[at + 1][s - FAR_FIRST]
+    return refs[which][s] if which < 3 else refs[3 + s // PART][s % PART]
 
 
 def column_of(meta_ref, which, s):
@@ -273,7 +270,7 @@
     places = jnp.stack([here + core, here + 1 - core, there + core, there + 1 - core]).astype(jnp.int32)
     places = jnp.concatenate([places, jnp.zeros((12,), jnp.int32)])[None]
 
-    def first_adjoint(received, own_last):
+    def first_adjoint(received, own):
         pair_meta = jnp.concatenate([pair_slots, pair_slots, places])
         kept, square, sent = apply_tiles(
             first_adjoint_kernel,
@@ -282,8 +279,8 @@
             4, TILE_COLS, CORE_CHANS, pair_meta, received, pair,
         )
         arrived = lax.ppermute(sent, "yh", swap)
-        own_last, *_ = lax.optimization_barrier((own_last, arrived, rewards_arrived, far_slots))
-        far = lax.ppermute(own_last, "yh", swap)
+        own, *_ = lax.optimization_barrier((own, arrived, rewards_arrived, far_slots))
+        far = lax.ppermute(own, "yh", swap)
         out = pl.pallas_call(
             combine_kernel,
             out_shape=message(TILE_COLS),
@@ -363,16 +360,13 @@
         compiler_params=LIMIT,
         name="first",
     )(jnp.concatenate([rewards_kept, rewards_sent], axis=1))
-    own_first, _ = lax.optimization_barrier((own[:FAR_FIRST], sends))
-    far_first = lax.ppermute(own_first, "yh", swap)
     received = lax.all_to_all(sends, COLS, 0, 0)
     meta = jnp.concatenate([pair_slots, far_slots, places])
     rewards_own = in_order(yh, rewards_kept, rewards_arrived, 0)
-    sends, far_last = first_adjoint(received, own[FAR_FIRST:])
+    sends, far = first_adjoint(received, own)
     raw, unit, beta_rows, sends = adjoint_end(lax.all_to_all(sends, "z", 0, 0), rewards_own, None)
-    far_last, _ = lax.optimization_barrier((far_last, sends))
-    far = [far_first, far_last]
-    tiles = pair + far + [lax.ppermute(part, "core", swap) for part in far]
+    far, _ = lax.optimization_barrier((far, sends))
+    tiles = pair + [far] + [lax.ppermute(part, "core", swap) for part in (far[:PART], far[PART:])]
     raws, alphas, betas = [raw], [], [beta_rows[0]]
     for iteration in range(ITERS):
         received = forward(lax.all_to_all(sends, "z", 0, 0))

time: 213 us -> 201 us (0.944)
  waiting for transfers between devices: 62.2 us -> 55.7 us
  blocking collectives: 58 us -> 54 us
    all_to_all x1, waiting for transfers between devices: 14.9 us -> 7.78 us  [shards(): received = forward(lax.all_to_all(sends, 'z', 0, 0))]
    all_to_all x1, waiting for transfers between devices: 5.89 us -> 2 us  [last_end(): lax.all_to_all(spread, ('yh', 'z', 'x', 'yl'), 0, 0)]
    ppermute x1, starting transfers between devices: 6.54 us -> 10.4 us  [last_end(): rows = in_order(core, rows, lax.ppermute(rows, 'core', swap), 1)]
    all_to_all x1, starting transfers between devices: 9.15 us -> 6.17 us  [last_end(): lax.all_to_all(spread, ('yh', 'z', 'x', 'yl'), 0, 0)]
    ppermute x2, starting transfers between devices: 8.09 us -> 10.9 us  [send_home(): arrived = lax.ppermute(jnp.concatenate([sent, rows]), name, swap)]
    ppermute x1, waiting for transfers between devices: 8.74 us -> 11.2 us  [shards(): far_slots = lax.ppermute(pair_slots, 'yh', swap)]
    ppermute x4 -> x3, starting transfers between devices: 6.93 us -> 4.7 us  [the longest x2 3.1 us: shards(): lax.ppermute(part, 'core', swap)]
    all_to_all x1, blocking collectives: 17.1 us -> 14.9 us  [adjoint(): return lax.all_to_all(out, 'z', 0, 0)]
  transfers between devices with their start and end apart: 18 -> 17, of which waited for: 11 -> 10; matrix products, arithmetic and copies ran while one was open for 2% -> 1% of each run, Pallas kernels for 1% -> 1%
where the time goes in v3:
time: 201 us; the launch traced here: 200 us
  starting transfers between devices  61 us (30%)
  waiting for transfers between devices  55.7 us (28%)
  blocking collectives  54 us (27%)
  Pallas kernels  18.4 us (9%)
  local copies, waits for them, and re-layouts  7.07 us (4%)
    all_to_all x1, waiting for transfers between devices, shards(): lax.all_to_all(sends, 'z', 0, 0)  15.5 us
    pallas_call x4, Pallas kernels, apply_tiles(): pl.pallas_call(kernel, out_shape=outs, in_specs=[SMEM] + [VMEM] * (1 + le...  15.2 us
    all_to_all x1, blocking collectives, shards(): received = forward(lax.all_to_all(sends, 'z', 0, 0))  15 us
    all_to_all x1, blocking collectives, adjoint(): return lax.all_to_all(out, 'z', 0, 0)  14.9 us
    all_to_all x1, blocking collectives, forward(): return lax.all_to_all(out, COLS, 0, 0)  13.8 us
    ppermute x1, waiting for transfers between devices, shards(): far_slots = lax.ppermute(pair_slots, 'yh', swap)  11.2 us
    ppermute x2, starting transfers between devices, send_home(): arrived = lax.ppermute(jnp.concatenate([sent, rows]), name, swap)  10.9 us
    ppermute x1, starting transfers between devices, last_end(): rows = in_order(core, rows, lax.ppermute(rows, 'core', swap), 1)  10.4 us
  transfers between devices with their start and end apart: 17, of which 10 were waited for; matrix products, arithmetic and copies ran while one was open for 1% of the time, Pallas kernels for 1%

profile of v3, /device:TPU:1, one launch (start us, length us, event | category | flops | bytes accessed | tf_op | source)
XLA Modules:
  0.0 199.6 jit_solution(14511124515506009969)
XLA Ops:
  0.6 3.3 %collective-permute-start.2 = (bf16[12,256,256]{2,1,0:T(8,128)(2,1)}, bf16[12,256,256]{2,1,0:T(8,128)(2,1)S(1)}, u32[]{:S(2)}, u32[]{:S(2)}) collective-permute-start(bf16[12,256,256]{2,1,0:T(8,128)(2,1)} %bitcast.31), channel_id=1, source_target_pairs={{0,8},{8,0},{1,9},{9,1},{2,10},{10,2},{3,11},{11,3},{4,12},{12,4},... | collective-permute-start | bytes 4718600 | tf_op jit(solution)/shard_map/ppermute | solution.py:266
  5.1 2.0 %collective-permute-done.1 = f32[64,256]{1,0:T(8,128)S(1)} collective-permute-done((f32[64,256]{1,0:T(8,128)S(1)}, f32[64,256]{1,0:T(8,128)S(1)}, u32[]{:S(2)}, u32[]{:S(2)}) %collective-permute-start.1) | collective-permute-done | bytes 65568 | tf_op jit(solution)/shard_map/ppermute | solution.py:258
  8.1 4.2 %all-to-all-start = ((s16[8,144,256]{2,1,0:T(8,128)(2,1)}), s16[8,144,256]{2,1,0:T(8,128)(2,1)}, u32[]{:S(2)}, u32[]{:S(2)}) async-start(s16[8,144,256]{2,1,0:T(8,128)(2,1)} %copy-done.4), calls=%async_computation | async-start | bytes 1179648 | tf_op jit(solution)/shard_map/all_to_all | solution.py:363
  14.3 7.9 %all-to-all-done.msg_ref = s16[8,144,256]{2,1,0:T(8,128)(2,1)} async-done(((s16[8,144,256]{2,1,0:T(8,128)(2,1)}), s16[8,144,256]{2,1,0:T(8,128)(2,1)}, u32[]{:S(2)}, u32[]{:S(2)}) %all-to-all-start) | async-done | bytes 589856 | tf_op jit(solution)/shard_map/all_to_all | solution.py:363
  22.2 4.0 %first_adjoint.1 = (f32[8,256,128]{2,1,0:T(8,128)S(1)}, f32[8,128]{1,0:T(8,128)S(1)}, s16[8,272,128]{2,1,0:T(8,128)(2,1)S(1)}) custom-call(s32[5,16]{1,0:T(8,128)S(1)} %concatenate.65.meta_ref, s16[8,144,256]{2,1,0:T(8,128)(2,1)} %all-to-all-done.msg_ref, bf16[12,256,256]{2,1,0:T(8,128)(2,1)S(1)} %bitcast.32, ...), custom_call_target="tpu_custom_call" | custom-call | flops 1610612736 | bytes 6291456 | tf_op jit(solution)/shard_map/first_adjoint/pallas_call | solution.py:229
  26.3 1.8 collective-permute-start.3
  28.0 1.3 collective-permute-start.4
  29.4 1.7 collective-permute-start.5
  31.0 11.2 %collective-permute-done.5 = s32[2,16]{1,0:T(2,128)S(1)} collective-permute-done((s32[2,16]{1,0:T(2,128)S(1)}, s32[2,16]{1,0:T(2,128)S(1)}, u32[]{:S(2)}, u32[]{:S(2)}) %collective-permute-start.5) | collective-permute-done | bytes 160 | tf_op jit(solution)/shard_map/ppermute | solution.py:268
  42.2 1.6 collective-permute-start.6
  45.0 8.2 %all-to-all-start.1 = ((s16[8,272,128]{2,1,0:T(8,128)(2,1)}), s16[8,272,128]{2,1,0:T(8,128)(2,1)}, u32[]{:S(2)}, u32[]{:S(2)}) async-start(s16[8,272,128]{2,1,0:T(8,128)(2,1)} %copy-done.6), calls=%async_computation.1 | async-start | bytes 1114112 | tf_op jit(solution)/shard_map/all_to_all | solution.py:367
  53.2 15.5 %all-to-all-done.1.msg_ref = s16[8,272,128]{2,1,0:T(8,128)(2,1)} async-done(((s16[8,272,128]{2,1,0:T(8,128)(2,1)}), s16[8,272,128]{2,1,0:T(8,128)(2,1)}, u32[]{:S(2)}, u32[]{:S(2)}) %all-to-all-start.1) | async-done | bytes 557088 | tf_op jit(solution)/shard_map/all_to_all | solution.py:367
  68.7 1.3 adjoint_end.2
  70.8 4.2 %all-to-all-start.2 = ((s16[8,272,128]{2,1,0:T(8,128)(2,1)}), s16[8,272,128]{2,1,0:T(8,128)(2,1)}, u32[]{:S(2)}, u32[]{:S(2)}) async-start(s16[8,272,128]{2,1,0:T(8,128)(2,1)} %copy-done.7), calls=%async_computation.2 | async-start | bytes 1114112 | tf_op jit(solution)/shard_map/all_to_all | solution.py:372
  75.1 2.5 %collective-permute-done.6.refs_2_ = bf16[12,256,256]{2,1,0:T(8,128)(2,1)S(1)} collective-permute-done((bf16[12,256,256]{2,1,0:T(8,128)(2,1)S(1)}, bf16[12,256,256]{2,1,0:T(8,128)(2,1)S(1)}, u32[]{:S(2)}, u32[]{:S(2)}) %collective-permute-start.6) | collective-permute-done | bytes 1572896 | tf_op jit(solution)/shard_map/ppermute | solution.py:283
  78.8 3.1 %collective-permute-start.8 = (bf16[6,256,256]{2,1,0:T(8,128)(2,1)}, bf16[6,256,256]{2,1,0:T(8,128)(2,1)}, u32[]{:S(2)}, u32[]{:S(2)}) collective-permute-start(bf16[6,256,256]{2,1,0:T(8,128)(2,1)} %get-tuple-element.38), channel_id=1, source_target_pairs={{0,8},{8,0},{1,9},{9,1},{2,10},{10,2},{3,11},{11,3},{4,12},{12,4},... | collective-permute-start | bytes 2359304 | tf_op jit(solution)/shard_map/ppermute | solution.py:369
  81.9 7.8 %all-to-all-done.2.msg_ref = s16[8,272,128]{2,1,0:T(8,128)(2,1)} async-done(((s16[8,272,128]{2,1,0:T(8,128)(2,1)}), s16[8,272,128]{2,1,0:T(8,128)(2,1)}, u32[]{:S(2)}, u32[]{:S(2)}) %all-to-all-start.2) | async-done | bytes 557088 | tf_op jit(solution)/shard_map/all_to_all | solution.py:372
  89.7 1.4 copy-done.2
  91.1 3.8 %forward.2 = s16[8,272,128]{2,1,0:T(8,128)(2,1)S(1)} custom-call(s32[5,16]{1,0:T(8,128)S(1)} %pad_add_fusion.meta_ref, s16[8,272,128]{2,1,0:T(8,128)(2,1)} %all-to-all-done.2.msg_ref, bf16[12,256,256]{2,1,0:T(8,128)(2,1)S(1)} %bitcast.34, bf16[12,256,256]{2,1,0:T(8,128)(2,1)S(1)} %copy-done.2, bf16[12,256,256]{2,1,0:T(8,128)(2,1)S(1)} %collective-permute-done.6.refs_2_, ...), custom_call_target="tpu_custom_call" | custom-call | flops 1610612736 | bytes 6291456 | tf_op jit(solution)/shard_map/forward/pallas_call | solution.py:229
  94.9 13.8 %all_to_all.47.msg_ref = s16[8,272,128]{2,1,0:T(8,128)(2,1)S(1)} all-to-all(s16[8,272,128]{2,1,0:T(8,128)(2,1)S(1)} %forward.2), channel_id=1, replica_groups=mesh['z'=8,'yh'=2,'core'=2,'x'=4,'yl'=2] {'x','yl'}, dimensions={0} | all-to-all | bytes 1114112 | tf_op jit(solution)/shard_map/all_to_all | solution.py:302
  109.0 10.4 %all_to_all.48.msg_ref = s16[8,272,128]{2,1,0:T(8,128)(2,1)S(1)} all-to-all(s16[8,272,128]{2,1,0:T(8,128)(2,1)S(1)} %get-tuple-element.27), channel_id=1, replica_groups=mesh['z'=8,'yh'=2,'core'=2,'x'=4,'yl'=2] {'x','yl'}, dimensions={0} | all-to-all | bytes 1114112 | tf_op jit(solution)/shard_map/all_to_all | solution.py:377
  119.4 3.7 %adjoint.1 = s16[8,272,128]{2,1,0:T(8,128)(2,1)S(1)} custom-call(s32[5,16]{1,0:T(8,128)S(1)} %pad_add_fusion.meta_ref, s16[8,272,128]{2,1,0:T(8,128)(2,1)S(1)} %all_to_all.48.msg_ref, bf16[12,256,256]{2,1,0:T(8,128)(2,1)S(1)} %bitcast.35, bf16[12,256,256]{2,1,0:T(8,128)(2,1)S(1)} %copy-done.3, bf16[12,256,256]{2,1,0:T(8,128)(2,1)S(1)} %collective-permute-done.6.refs_2_, ...), custom_call_target="tpu_custom_call" | custom-call | flops 1610612736 | bytes 6291456 | tf_op jit(solution)/shard_map/adjoint/pallas_call | solution.py:229
  123.1 14.9 %all_to_all.49.msg_ref = s16[8,272,128]{2,1,0:T(8,128)(2,1)S(1)} all-to-all(s16[8,272,128]{2,1,0:T(8,128)(2,1)S(1)} %adjoint.1), channel_id=1, replica_groups=mesh['z'=8,'yh'=2,'core'=2,'x'=4,'yl'=2] {'z'}, dimensions={0} | all-to-all | bytes 1114112 | tf_op jit(solution)/shard_map/all_to_all | solution.py:298
  138.3 15.0 %all_to_all.50.msg_ref = s16[8,272,128]{2,1,0:T(8,128)(2,1)S(1)} all-to-all(s16[8,272,128]{2,1,0:T(8,128)(2,1)S(1)} %get-tuple-element.34), channel_id=1, replica_groups=mesh['z'=8,'yh'=2,'core'=2,'x'=4,'yl'=2] {'z'}, dimensions={0} | all-to-all | bytes 1114112 | tf_op jit(solution)/shard_map/all_to_all | solution.py:372
  153.3 3.6 %forward.3 = s16[8,272,128]{2,1,0:T(8,128)(2,1)S(1)} custom-call(s32[5,16]{1,0:T(8,128)S(1)} %pad_add_fusion.meta_ref, s16[8,272,128]{2,1,0:T(8,128)(2,1)S(1)} %all_to_all.50.msg_ref, bf16[12,256,256]{2,1,0:T(8,128)(2,1)S(1)} %bitcast.36, bf16[12,256,256]{2,1,0:T(8,128)(2,1)S(1)} %copy-done.3, bf16[12,256,256]{2,1,0:T(8,128)(2,1)S(1)} %collective-permute-done.6.refs_2_, ...), custom_call_target="tpu_custom_call" | custom-call | flops 1610612736 | bytes 6291456 | tf_op jit(solution)/shard_map/forward/pallas_call | solution.py:229
  157.7 3.5 %all-to-all-start.7 = ((s16[8,272,128]{2,1,0:T(8,128)(2,1)}), s16[8,272,128]{2,1,0:T(8,128)(2,1)S(1)}, u32[]{:S(2)}, u32[]{:S(2)}) async-start(s16[8,272,128]{2,1,0:T(8,128)(2,1)} %copy-done.5), calls=%async_computation.7 | async-start | bytes 1114112 | tf_op jit(solution)/shard_map/all_to_all | solution.py:302
  161.4 1.6 collective-permute-start.9
  163.1 5.4 %all-to-all-done.7.msg_ref = s16[8,272,128]{2,1,0:T(8,128)(2,1)S(1)} async-done(((s16[8,272,128]{2,1,0:T(8,128)(2,1)}), s16[8,272,128]{2,1,0:T(8,128)(2,1)S(1)}, u32[]{:S(2)}, u32[]{:S(2)}) %all-to-all-start.7) | async-done | bytes 557088 | tf_op jit(solution)/shard_map/all_to_all | solution.py:302
  169.3 6.2 %all-to-all-start.8 = ((f32[128,2,128]{2,1,0:T(2,128)}), f32[128,2,128]{2,1,0:T(2,128)S(1)}, u32[]{:S(2)}, u32[]{:S(2)}) async-start(f32[128,2,128]{2,1,0:T(2,128)} %last_end.1), calls=%async_computation.8 | async-start | bytes 262144 | tf_op jit(solution)/shard_map/all_to_all | solution.py:334
  175.6 9.3 %collective-permute-start.10 = (f32[136,256]{1,0:T(8,128)S(1)}, f32[136,256]{1,0:T(8,128)S(1)}, u32[]{:S(2)}, u32[]{:S(2)}) collective-permute-start(f32[136,256]{1,0:T(8,128)S(1)} %pad_maximum_fusion), channel_id=1, source_target_pairs={{0,8},{8,0},{1,9},{9,1},{2,10},{10,2},{3,11},{11,3},{4,12},{12,4},... | collective-permute-start | bytes 417800 | tf_op jit(solution)/shard_map/ppermute | solution.py:349
  184.9 2.0 %all-to-all-done.8 = f32[128,2,128]{2,1,0:T(2,128)S(1)} async-done(((f32[128,2,128]{2,1,0:T(2,128)}), f32[128,2,128]{2,1,0:T(2,128)S(1)}, u32[]{:S(2)}, u32[]{:S(2)}) %all-to-all-start.8) | async-done | bytes 131104 | tf_op jit(solution)/shard_map/all_to_all | solution.py:334
  187.0 10.4 %collective-permute-start.11 = (f32[2,256]{1,0:T(2,128)S(1)}, f32[2,256]{1,0:T(2,128)S(1)}, u32[]{:S(2)}, u32[]{:S(2)}) collective-permute-start(f32[2,256]{1,0:T(2,128)S(1)} %pad_maximum_fusion.2), channel_id=1, source_target_pairs={{0,8},{8,0},{1,9},{9,1},{2,10},{10,2},{3,11},{11,3},{4,12},{12,4},... | collective-permute-start | bytes 6152 | tf_op jit(solution)/shard_map/ppermute | solution.py:336
  (77 shorter events, 11.4 us)
Async XLA Ops:
  0.6 21.6 %copy-start = (bf16[1,1,12,256,256]{4,3,2,1,0:T(8,128)(2,1)S(1)}, bf16[1,1,12,256,256]{4,3,2,1,0:T(8,128)(2,1)}, u32[]{:S(2)}) copy-start(bf16[1,1,12,256,256]{4,3,2,1,0:T(8,128)(2,1)} %param.5) | copy-start | bytes 4718596
  0.6 12.3 %copy-start.10 = (s32[1,1,12]{2,1,0:T(1,128)S(1)}, s32[1,1,12]{2,1,0:T(1,128)}, u32[]{:S(2)}) copy-start(s32[1,1,12]{2,1,0:T(1,128)} %param.6) | copy-start | bytes 148
  0.6 21.6 %collective-permute-start.2 = (bf16[12,256,256]{2,1,0:T(8,128)(2,1)}, bf16[12,256,256]{2,1,0:T(8,128)(2,1)S(1)}, u32[]{:S(2)}, u32[]{:S(2)}) collective-permute-start(bf16[12,256,256]{2,1,0:T(8,128)(2,1)} %bitcast.31), channel_id=1, source_target_pairs={{0,8},{8,0},{1,9},{9,1},{2,10},{10,2},{3,11},{11,3},{4,12},{12,4},... | collective-permute-start | bytes 4718600 | tf_op jit(solution)/shard_map/ppermute | solution.py:266
  4.9 2.2 %collective-permute-start.1 = (f32[64,256]{1,0:T(8,128)S(1)}, f32[64,256]{1,0:T(8,128)S(1)}, u32[]{:S(2)}, u32[]{:S(2)}) collective-permute-start(f32[64,256]{1,0:T(8,128)S(1)} %get-tuple-element.50), channel_id=1, source_target_pairs={{0,8},{8,0},{1,9},{9,1},{2,10},{10,2},{3,11},{11,3},{4,12},{12,4},... | collective-permute-start | bytes 196616 | tf_op jit(solution)/shard_map/ppermute | solution.py:258
  7.3 0.8 copy-start.4
  8.1 14.1 %all-to-all-start = ((s16[8,144,256]{2,1,0:T(8,128)(2,1)}), s16[8,144,256]{2,1,0:T(8,128)(2,1)}, u32[]{:S(2)}, u32[]{:S(2)}) async-start(s16[8,144,256]{2,1,0:T(8,128)(2,1)} %copy-done.4), calls=%async_computation | async-start | bytes 1179648 | tf_op jit(solution)/shard_map/all_to_all | solution.py:363
  13.0 1.2 collective-permute-start
  13.6 12.7 %copy-start.8 = (s32[16]{0:T(128)}, s32[16]{0:T(128)S(1)}, u32[]{:S(2)}) copy-start(s32[16]{0:T(128)S(1)} %concatenate.64) | copy-start | bytes 196
  22.2 4.1 %copy-start.1 = (bf16[12,256,256]{2,1,0:T(8,128)(2,1)}, bf16[12,256,256]{2,1,0:T(8,128)(2,1)S(1)}, u32[]{:S(2)}) copy-start(bf16[12,256,256]{2,1,0:T(8,128)(2,1)S(1)} %collective-permute-done.2.refs_1_) | copy-start | bytes 4718596
  26.3 15.9 %collective-permute-start.3 = (s16[8,272,128]{2,1,0:T(8,128)(2,1)S(1)}, s16[8,272,128]{2,1,0:T(8,128)(2,1)S(1)}, u32[]{:S(2)}, u32[]{:S(2)}) collective-permute-start(s16[8,272,128]{2,1,0:T(8,128)(2,1)S(1)} %get-tuple-element.21), channel_id=1, source_target_pairs={{0,16},{16,0},{1,17},{17,1},{2,18},{18,2},{3,19},{19,3},{4,20},{20... | collective-permute-start | bytes 1671176 | tf_op jit(solution)/shard_map/ppermute | solution.py:281
  28.0 14.2 %collective-permute-start.4 = (f32[128,128]{1,0:T(8,128)S(1)}, f32[128,128]{1,0:T(8,128)S(1)}, u32[]{:S(2)}, u32[]{:S(2)}) collective-permute-start(f32[128,128]{1,0:T(8,128)S(1)} %get-tuple-element.48), channel_id=1, source_target_pairs={{0,16},{16,0},{1,17},{17,1},{2,18},{18,2},{3,19},{19,3},{4,20},{20... | collective-permute-start | bytes 196616 | tf_op jit(solution)/shard_map/ppermute | solution.py:265
  29.4 12.9 %collective-permute-start.5 = (s32[2,16]{1,0:T(2,128)S(1)}, s32[2,16]{1,0:T(2,128)S(1)}, u32[]{:S(2)}, u32[]{:S(2)}) collective-permute-start(s32[2,16]{1,0:T(2,128)S(1)} %pad_add_fusion.1), channel_id=1, source_target_pairs={{0,16},{16,0},{1,17},{17,1},{2,18},{18,2},{3,19},{19,3},{4,20},{20... | collective-permute-start | bytes 392 | tf_op jit(solution)/shard_map/ppermute | solution.py:268
  42.2 2.8 %copy-start.11 = (s32[2,16]{1,0:T(2,128)}, s32[2,16]{1,0:T(2,128)S(1)}, u32[]{:S(2)}) copy-start(s32[2,16]{1,0:T(2,128)S(1)} %collective-permute-done.5) | copy-start | bytes 388
  42.2 35.3 %collective-permute-start.6 = (bf16[12,256,256]{2,1,0:T(8,128)(2,1)S(1)}, bf16[12,256,256]{2,1,0:T(8,128)(2,1)S(1)}, u32[]{:S(2)}, u32[]{:S(2)}) collective-permute-start(bf16[12,256,256]{2,1,0:T(8,128)(2,1)S(1)} %bitcast.33), channel_id=1, source_target_pairs={{0,16},{16,0},{1,17},{17,1},{2,18},{18,2},{3,19},{19,3},{4,20},{20... | collective-permute-start | bytes 4718600 | tf_op jit(solution)/shard_map/ppermute | solution.py:283
  44.2 0.8 copy-start.6
  45.0 23.7 %all-to-all-start.1 = ((s16[8,272,128]{2,1,0:T(8,128)(2,1)}), s16[8,272,128]{2,1,0:T(8,128)(2,1)}, u32[]{:S(2)}, u32[]{:S(2)}) async-start(s16[8,272,128]{2,1,0:T(8,128)(2,1)} %copy-done.6), calls=%async_computation.1 | async-start | bytes 1114112 | tf_op jit(solution)/shard_map/all_to_all | solution.py:367
  70.0 0.8 copy-start.7
  70.8 18.8 %all-to-all-start.2 = ((s16[8,272,128]{2,1,0:T(8,128)(2,1)}), s16[8,272,128]{2,1,0:T(8,128)(2,1)}, u32[]{:S(2)}, u32[]{:S(2)}) async-start(s16[8,272,128]{2,1,0:T(8,128)(2,1)} %copy-done.7), calls=%async_computation.2 | async-start | bytes 1114112 | tf_op jit(solution)/shard_map/all_to_all | solution.py:372
  75.0 6.8 %copy-start.9 = (s32[16]{0:T(128)S(1)}, s32[16]{0:T(128)}, u32[]{:S(2)}) copy-start(s32[16]{0:T(128)} %copy-done.8) | copy-start | bytes 196
  75.0 6.8 %copy-start.12 = (s32[2,16]{1,0:T(2,128)S(1)}, s32[2,16]{1,0:T(2,128)}, u32[]{:S(2)}) copy-start(s32[2,16]{1,0:T(2,128)} %copy-done.11) | copy-start | bytes 388
  78.8 10.9 %collective-permute-start.8 = (bf16[6,256,256]{2,1,0:T(8,128)(2,1)}, bf16[6,256,256]{2,1,0:T(8,128)(2,1)}, u32[]{:S(2)}, u32[]{:S(2)}) collective-permute-start(bf16[6,256,256]{2,1,0:T(8,128)(2,1)} %get-tuple-element.38), channel_id=1, source_target_pairs={{0,8},{8,0},{1,9},{9,1},{2,10},{10,2},{3,11},{11,3},{4,12},{12,4},... | collective-permute-start | bytes 2359304 | tf_op jit(solution)/shard_map/ppermute | solution.py:369
  81.9 7.8 %collective-permute-start.7 = (bf16[6,256,256]{2,1,0:T(8,128)(2,1)}, bf16[6,256,256]{2,1,0:T(8,128)(2,1)}, u32[]{:S(2)}, u32[]{:S(2)}) collective-permute-start(bf16[6,256,256]{2,1,0:T(8,128)(2,1)} %get-tuple-element.39), channel_id=1, source_target_pairs={{0,8},{8,0},{1,9},{9,1},{2,10},{10,2},{3,11},{11,3},{4,12},{12,4},... | collective-permute-start | bytes 2359304 | tf_op jit(solution)/shard_map/ppermute | solution.py:369
  89.7 1.4 copy-start.2
  94.9 24.5 %copy-start.3 = (bf16[12,256,256]{2,1,0:T(8,128)(2,1)S(1)}, bf16[12,256,256]{2,1,0:T(8,128)(2,1)}, u32[]{:S(2)}) copy-start(bf16[12,256,256]{2,1,0:T(8,128)(2,1)} %copy-done.1) | copy-start | bytes 4718596
  156.9 0.8 copy-start.5
  157.7 10.7 %all-to-all-start.7 = ((s16[8,272,128]{2,1,0:T(8,128)(2,1)}), s16[8,272,128]{2,1,0:T(8,128)(2,1)S(1)}, u32[]{:S(2)}, u32[]{:S(2)}) async-start(s16[8,272,128]{2,1,0:T(8,128)(2,1)} %copy-done.5), calls=%async_computation.7 | async-start | bytes 1114112 | tf_op jit(solution)/shard_map/all_to_all | solution.py:302
  161.4 14.1 %collective-permute-start.9 = (f32[264,128]{1,0:T(8,128)S(1)}, f32[264,128]{1,0:T(8,128)S(1)}, u32[]{:S(2)}, u32[]{:S(2)}) collective-permute-start(f32[264,128]{1,0:T(8,128)S(1)} %concatenate.73), channel_id=1, source_target_pairs={{0,16},{16,0},{1,17},{17,1},{2,18},{18,2},{3,19},{19,3},{4,20},{20... | collective-permute-start | bytes 405512 | tf_op jit(solution)/shard_map/ppermute | solution.py:349
  169.3 17.6 %all-to-all-start.8 = ((f32[128,2,128]{2,1,0:T(2,128)}), f32[128,2,128]{2,1,0:T(2,128)S(1)}, u32[]{:S(2)}, u32[]{:S(2)}) async-start(f32[128,2,128]{2,1,0:T(2,128)} %last_end.1), calls=%async_computation.8 | async-start | bytes 262144 | tf_op jit(solution)/shard_map/all_to_all | solution.py:334
  175.6 21.8 %collective-permute-start.10 = (f32[136,256]{1,0:T(8,128)S(1)}, f32[136,256]{1,0:T(8,128)S(1)}, u32[]{:S(2)}, u32[]{:S(2)}) collective-permute-start(f32[136,256]{1,0:T(8,128)S(1)} %pad_maximum_fusion), channel_id=1, source_target_pairs={{0,8},{8,0},{1,9},{9,1},{2,10},{10,2},{3,11},{11,3},{4,12},{12,4},... | collective-permute-start | bytes 417800 | tf_op jit(solution)/shard_map/ppermute | solution.py:349
  187.0 11.3 %collective-permute-start.11 = (f32[2,256]{1,0:T(2,128)S(1)}, f32[2,256]{1,0:T(2,128)S(1)}, u32[]{:S(2)}, u32[]{:S(2)}) collective-permute-start(f32[2,256]{1,0:T(2,128)S(1)} %pad_maximum_fusion.2), channel_id=1, source_target_pairs={{0,8},{8,0},{1,9},{9,1},{2,10},{10,2},{3,11},{11,3},{4,12},{12,4},... | collective-permute-start | bytes 6152 | tf_op jit(solution)/shard_map/ppermute | solution.py:336

commit v4 on v3

--- a/solution.py
+++ b/solution.py
@@ -117,15 +117,16 @@
         store_message(out_ref, k, sum_ref[k], square)
 
 
-def adjoint_sums(meta_ref, msg_ref, tile_refs, vec_ref, sum_ref):
-    chans = msg_ref.shape[-1]
+def adjoint_sums(meta_ref, msg_ref, tile_refs, vec_ref, sum_ref, first=0):
+    chans = sum_ref.shape[-1]
+    lanes = slice(first, first + chans)
     blocks = msg_ref.shape[1] // STATES_DEV
     square = jnp.zeros((1, chans), F32)
     for k in range(N_COLS):
-        step, part = read_head(msg_ref[k, blocks * STATES_DEV :, :])
+        step, part = read_head(msg_ref[k, blocks * STATES_DEV :, lanes])
         square = square + part
         for block in range(blocks):
-            values = wide(msg_ref[k, block * STATES_DEV : (block + 1) * STATES_DEV, :]) * step
+            values = wide(msg_ref[k, block * STATES_DEV : (block + 1) * STATES_DEV, lanes]) * step
             split_store(vec_ref, block * 2 + k // 4, pl.ds((k % 4) * STATES_DEV, STATES_DEV), values)
     sum_ref[...] = jnp.zeros_like(sum_ref)
     for which in range(blocks):
@@ -148,13 +149,19 @@
         store_message(out_ref, k, sum_ref[k], square)
 
 
-def first_adjoint_kernel(meta_ref, msg_ref, *refs):
-    tile_refs, (kept_ref, square_ref, out_ref, vec_ref, sum_ref) = refs[:-5], refs[-5:]
+def sent_adjoint_kernel(meta_ref, msg_ref, *refs):
+    tile_refs, (out_ref, vec_ref, sum_ref) = refs[:-3], refs[-3:]
+    square = adjoint_sums(meta_ref, msg_ref, tile_refs, vec_ref, sum_ref, CHANS)
+    for k in range(TILE_COLS):
+        store_message(out_ref, k, sum_ref[k], square)
+
+
+def kept_adjoint_kernel(meta_ref, msg_ref, *refs):
+    tile_refs, (kept_ref, square_ref, vec_ref, sum_ref) = refs[:-4], refs[-4:]
     square = adjoint_sums(meta_ref, msg_ref, tile_refs, vec_ref, sum_ref)
-    square_ref[...] = jnp.broadcast_to(square[:, :CHANS], square_ref.shape)
+    square_ref[...] = jnp.broadcast_to(square, square_ref.shape)
     for k in range(TILE_COLS):
-        kept_ref[k] = sum_ref[k, :, :CHANS]
-        store_message(out_ref, k, sum_ref[k, :, CHANS:], square[:, CHANS:])
+        kept_ref[k] = sum_ref[k]
 
 
 def combine_kernel(kept_ref, square_ref, msg_ref, out_ref):
@@ -272,14 +279,18 @@
 
     def first_adjoint(received, own):
         pair_meta = jnp.concatenate([pair_slots, pair_slots, places])
-        kept, square, sent = apply_tiles(
-            first_adjoint_kernel,
-            "first_adjoint",
-            (f32(TILE_COLS, TILE, CHANS), f32(8, CHANS), message(TILE_COLS)),
-            4, TILE_COLS, CORE_CHANS, pair_meta, received, pair,
+        sent = apply_tiles(
+            sent_adjoint_kernel, "sent_adjoint", message(TILE_COLS), 4, TILE_COLS, CHANS, pair_meta, received, pair
+        )
+        received, sent = lax.optimization_barrier((received, sent))
+        kept, square = apply_tiles(
+            kept_adjoint_kernel,
+            "kept_adjoint",
+            (f32(TILE_COLS, TILE, CHANS), f32(8, CHANS)),
+            4, TILE_COLS, CHANS, pair_meta, received, pair,
         )
         arrived = lax.ppermute(sent, "yh", swap)
-        own, *_ = lax.optimization_barrier((own, arrived, rewards_arrived, far_slots))
+        own, *_ = lax.optimization_barrier((own, arrived, kept))
         far = lax.ppermute(own, "yh", swap)
         out = pl.pallas_call(
             combine_kernel,
@@ -361,6 +372,7 @@
         name="first",
     )(jnp.concatenate([rewards_kept, rewards_sent], axis=1))
     received = lax.all_to_all(sends, COLS, 0, 0)
+    received, far_slots, rewards_arrived = lax.optimization_barrier((received, far_slots, rewards_arrived))
     meta = jnp.concatenate([pair_slots, far_slots, places])
     rewards_own = in_order(yh, rewards_kept, rewards_arrived, 0)
     sends, far = first_adjoint(received, own)

time: 201 us -> 200 us (level)
  waiting for transfers between devices: 55.7 us -> 52.4 us
    ppermute x1, waiting for transfers between devices: 0.01 us -> 11.2 us  [first_adjoint(): arrived = lax.ppermute(sent, 'yh', swap)]
    all_to_all x1, waiting for transfers between devices: 7.94 us -> 0.01 us  [shards(): received = lax.all_to_all(sends, COLS, 0, 0)]
    ppermute x1, waiting for transfers between devices: 11.2 us -> 5.85 us  [shards(): far_slots = lax.ppermute(pair_slots, 'yh', swap)]
    pallas_call x4 -> x5, Pallas kernels: 15.2 us -> 16.4 us  [apply_tiles(): pl.pallas_call(kernel, out_shape=outs, in_specs=[SMEM] + [VMEM] * (1 + le...]
  transfers between devices with their start and end apart: 17 -> 17, of which waited for: 10 -> 9; matrix products, arithmetic and copies ran while one was open for 1% -> 1% of each run, Pallas kernels for 1% -> 3%
where the time goes in v4:
time: 200 us; the launch traced here: 199 us
  starting transfers between devices  62 us (31%)
  blocking collectives  54.7 us (27%)
  waiting for transfers between devices  52.4 us (26%)
  Pallas kernels  19.6 us (10%)
  local copies, waits for them, and re-layouts  7.07 us (4%)
    pallas_call x5, Pallas kernels, apply_tiles(): pl.pallas_call(kernel, out_shape=outs, in_specs=[SMEM] + [VMEM] * (1 + le...  16.4 us
    all_to_all x1, waiting for transfers between devices, shards(): lax.all_to_all(sends, 'z', 0, 0)  15.5 us
    all_to_all x1, blocking collectives, adjoint(): return lax.all_to_all(out, 'z', 0, 0)  15 us
    all_to_all x1, blocking collectives, shards(): received = forward(lax.all_to_all(sends, 'z', 0, 0))  14.9 us
    all_to_all x1, blocking collectives, forward(): return lax.all_to_all(out, COLS, 0, 0)  14.6 us
    ppermute x2, starting transfers between devices, send_home(): arrived = lax.ppermute(jnp.concatenate([sent, rows]), name, swap)  12.4 us
    ppermute x1, waiting for transfers between devices, first_adjoint(): arrived = lax.ppermute(sent, 'yh', swap)  11.2 us
    ppermute x1, starting transfers between devices, last_end(): rows = in_order(core, rows, lax.ppermute(rows, 'core', swap), 1)  10.9 us
  transfers between devices with their start and end apart: 17, of which 9 were waited for; matrix products, arithmetic and copies ran while one was open for 1% of the time, Pallas kernels for 3%

profile of v4, /device:TPU:1, one launch (start us, length us, event | category | flops | bytes accessed | tf_op | source)
XLA Modules:
  0.0 199.2 jit_solution(15746410134087211827)
XLA Ops:
  0.6 3.3 %collective-permute-start.4 = (bf16[12,256,256]{2,1,0:T(8,128)(2,1)}, bf16[12,256,256]{2,1,0:T(8,128)(2,1)S(1)}, u32[]{:S(2)}, u32[]{:S(2)}) collective-permute-start(bf16[12,256,256]{2,1,0:T(8,128)(2,1)} %bitcast.31), channel_id=1, source_target_pairs={{0,8},{8,0},{1,9},{9,1},{2,10},{10,2},{3,11},{11,3},{4,12},{12,4},... | collective-permute-start | bytes 4718600 | tf_op jit(solution)/shard_map/ppermute | solution.py:273
  5.1 2.0 %collective-permute-done.1 = f32[64,256]{1,0:T(8,128)S(1)} collective-permute-done((f32[64,256]{1,0:T(8,128)S(1)}, f32[64,256]{1,0:T(8,128)S(1)}, u32[]{:S(2)}, u32[]{:S(2)}) %collective-permute-start.1) | collective-permute-done | bytes 65568 | tf_op jit(solution)/shard_map/ppermute | solution.py:265
  8.1 4.2 %all-to-all-start = ((s16[8,144,256]{2,1,0:T(8,128)(2,1)}), s16[8,144,256]{2,1,0:T(8,128)(2,1)}, u32[]{:S(2)}, u32[]{:S(2)}) async-start(s16[8,144,256]{2,1,0:T(8,128)(2,1)} %copy-done.4), calls=%async_computation | async-start | bytes 1179648 | tf_op jit(solution)/shard_map/all_to_all | solution.py:374
  13.6 2.0 %collective-permute-start.3 = (f32[128,128]{1,0:T(8,128)S(1)}, f32[128,128]{1,0:T(8,128)S(1)}, u32[]{:S(2)}, u32[]{:S(2)}) collective-permute-start(f32[128,128]{1,0:T(8,128)S(1)} %get-tuple-element.56), channel_id=1, source_target_pairs={{0,16},{16,0},{1,17},{17,1},{2,18},{18,2},{3,19},{19,3},{4,20},{20... | collective-permute-start | bytes 196616 | tf_op jit(solution)/shard_map/ppermute | solution.py:272
  16.7 5.8 %collective-permute-done.2 = s32[2,16]{1,0:T(2,128)S(1)} collective-permute-done((s32[2,16]{1,0:T(2,128)S(1)}, s32[2,16]{1,0:T(2,128)S(1)}, u32[]{:S(2)}, u32[]{:S(2)}) %collective-permute-start.2) | collective-permute-done | bytes 160 | tf_op jit(solution)/shard_map/ppermute | solution.py:275
  22.6 2.9 %sent_adjoint.1 = s16[8,272,128]{2,1,0:T(8,128)(2,1)S(1)} custom-call(s32[5,16]{1,0:T(8,128)S(1)} %concatenate.65.meta_ref, s16[8,144,256]{2,1,0:T(8,128)(2,1)} %all-to-all-done.msg_ref, bf16[12,256,256]{2,1,0:T(8,128)(2,1)S(1)} %bitcast.32, bf16[12,256,256]{2,1,0:T(8,128)(2,1)S(1)} %collective-permute-done.4.refs_1_), custom_call_target="tpu_custom_call" | custom-call | flops 1610612736 | bytes 6291456 | tf_op jit(solution)/shard_map/sent_adjoint/pallas_call | solution.py:236
  25.5 1.4 collective-permute-start.5
  26.9 2.3 %kept_adjoint.1 = (f32[8,256,128]{2,1,0:T(8,128)S(1)}, f32[8,128]{1,0:T(8,128)S(1)}) custom-call(s32[5,16]{1,0:T(8,128)S(1)} %concatenate.65.meta_ref, s16[8,144,256]{2,1,0:T(8,128)(2,1)} %all-to-all-done.msg_ref, bf16[12,256,256]{2,1,0:T(8,128)(2,1)S(1)} %bitcast.33, bf16[12,256,256]{2,1,0:T(8,128)(2,1)S(1)} %collective-permute-done.4.refs_1_), custom_call_target="tpu_custom_call" | custom-call | flops 1610612736 | bytes 6291456 | tf_op jit(solution)/shard_map/kept_adjoint/pallas_call | solution.py:236
  29.2 11.2 %collective-permute-done.5.msg_ref = s16[8,272,128]{2,1,0:T(8,128)(2,1)S(1)} collective-permute-done((s16[8,272,128]{2,1,0:T(8,128)(2,1)S(1)}, s16[8,272,128]{2,1,0:T(8,128)(2,1)S(1)}, u32[]{:S(2)}, u32[]{:S(2)}) %collective-permute-start.5) | collective-permute-done | bytes 557088 | tf_op jit(solution)/shard_map/ppermute | solution.py:292
  42.3 8.2 %all-to-all-start.1 = ((s16[8,272,128]{2,1,0:T(8,128)(2,1)}), s16[8,272,128]{2,1,0:T(8,128)(2,1)}, u32[]{:S(2)}, u32[]{:S(2)}) async-start(s16[8,272,128]{2,1,0:T(8,128)(2,1)} %copy-done.6), calls=%async_computation.1 | async-start | bytes 1114112 | tf_op jit(solution)/shard_map/all_to_all | solution.py:379
  50.5 15.5 %all-to-all-done.1.msg_ref = s16[8,272,128]{2,1,0:T(8,128)(2,1)} async-done(((s16[8,272,128]{2,1,0:T(8,128)(2,1)}), s16[8,272,128]{2,1,0:T(8,128)(2,1)}, u32[]{:S(2)}, u32[]{:S(2)}) %all-to-all-start.1) | async-done | bytes 557088 | tf_op jit(solution)/shard_map/all_to_all | solution.py:379
  66.1 1.3 adjoint_end.2
  68.2 4.2 %all-to-all-start.2 = ((s16[8,272,128]{2,1,0:T(8,128)(2,1)}), s16[8,272,128]{2,1,0:T(8,128)(2,1)}, u32[]{:S(2)}, u32[]{:S(2)}) async-start(s16[8,272,128]{2,1,0:T(8,128)(2,1)} %copy-done.7), calls=%async_computation.2 | async-start | bytes 1114112 | tf_op jit(solution)/shard_map/all_to_all | solution.py:384
  72.4 3.7 %collective-permute-done.6.refs_2_ = bf16[12,256,256]{2,1,0:T(8,128)(2,1)S(1)} collective-permute-done((bf16[12,256,256]{2,1,0:T(8,128)(2,1)S(1)}, bf16[12,256,256]{2,1,0:T(8,128)(2,1)S(1)}, u32[]{:S(2)}, u32[]{:S(2)}) %collective-permute-start.6) | collective-permute-done | bytes 1572896 | tf_op jit(solution)/shard_map/ppermute | solution.py:294
  76.1 1.2 fusion.5
  77.4 2.6 %collective-permute-start.8 = (bf16[6,256,256]{2,1,0:T(8,128)(2,1)}, bf16[6,256,256]{2,1,0:T(8,128)(2,1)}, u32[]{:S(2)}, u32[]{:S(2)}) collective-permute-start(bf16[6,256,256]{2,1,0:T(8,128)(2,1)} %get-tuple-element.46), channel_id=1, source_target_pairs={{0,8},{8,0},{1,9},{9,1},{2,10},{10,2},{3,11},{11,3},{4,12},{12,4},... | collective-permute-start | bytes 2359304 | tf_op jit(solution)/shard_map/ppermute | solution.py:381
  80.0 7.3 %all-to-all-done.2.msg_ref = s16[8,272,128]{2,1,0:T(8,128)(2,1)} async-done(((s16[8,272,128]{2,1,0:T(8,128)(2,1)}), s16[8,272,128]{2,1,0:T(8,128)(2,1)}, u32[]{:S(2)}, u32[]{:S(2)}) %all-to-all-start.2) | async-done | bytes 557088 | tf_op jit(solution)/shard_map/all_to_all | solution.py:384
  87.3 1.4 copy-done.2
  88.7 3.8 %forward.2 = s16[8,272,128]{2,1,0:T(8,128)(2,1)S(1)} custom-call(s32[5,16]{1,0:T(8,128)S(1)} %pad_add_fusion.meta_ref, s16[8,272,128]{2,1,0:T(8,128)(2,1)} %all-to-all-done.2.msg_ref, bf16[12,256,256]{2,1,0:T(8,128)(2,1)S(1)} %bitcast.35, bf16[12,256,256]{2,1,0:T(8,128)(2,1)S(1)} %copy-done.2, bf16[12,256,256]{2,1,0:T(8,128)(2,1)S(1)} %collective-permute-done.6.refs_2_, ...), custom_call_target="tpu_custom_call" | custom-call | flops 1610612736 | bytes 6291456 | tf_op jit(solution)/shard_map/forward/pallas_call | solution.py:236
  92.6 14.6 %all_to_all.47.msg_ref = s16[8,272,128]{2,1,0:T(8,128)(2,1)S(1)} all-to-all(s16[8,272,128]{2,1,0:T(8,128)(2,1)S(1)} %forward.2), channel_id=1, replica_groups=mesh['z'=8,'yh'=2,'core'=2,'x'=4,'yl'=2] {'x','yl'}, dimensions={0} | all-to-all | bytes 1114112 | tf_op jit(solution)/shard_map/all_to_all | solution.py:313
  107.4 10.3 %all_to_all.48.msg_ref = s16[8,272,128]{2,1,0:T(8,128)(2,1)S(1)} all-to-all(s16[8,272,128]{2,1,0:T(8,128)(2,1)S(1)} %get-tuple-element.35), channel_id=1, replica_groups=mesh['z'=8,'yh'=2,'core'=2,'x'=4,'yl'=2] {'x','yl'}, dimensions={0} | all-to-all | bytes 1114112 | tf_op jit(solution)/shard_map/all_to_all | solution.py:389
  117.7 3.7 %adjoint.1 = s16[8,272,128]{2,1,0:T(8,128)(2,1)S(1)} custom-call(s32[5,16]{1,0:T(8,128)S(1)} %pad_add_fusion.meta_ref, s16[8,272,128]{2,1,0:T(8,128)(2,1)S(1)} %all_to_all.48.msg_ref, bf16[12,256,256]{2,1,0:T(8,128)(2,1)S(1)} %bitcast.36, bf16[12,256,256]{2,1,0:T(8,128)(2,1)S(1)} %copy-done.3, bf16[12,256,256]{2,1,0:T(8,128)(2,1)S(1)} %collective-permute-done.6.refs_2_, ...), custom_call_target="tpu_custom_call" | custom-call | flops 1610612736 | bytes 6291456 | tf_op jit(solution)/shard_map/adjoint/pallas_call | solution.py:236
  121.4 15.0 %all_to_all.49.msg_ref = s16[8,272,128]{2,1,0:T(8,128)(2,1)S(1)} all-to-all(s16[8,272,128]{2,1,0:T(8,128)(2,1)S(1)} %adjoint.1), channel_id=1, replica_groups=mesh['z'=8,'yh'=2,'core'=2,'x'=4,'yl'=2] {'z'}, dimensions={0} | all-to-all | bytes 1114112 | tf_op jit(solution)/shard_map/all_to_all | solution.py:309
  136.7 14.9 %all_to_all.50.msg_ref = s16[8,272,128]{2,1,0:T(8,128)(2,1)S(1)} all-to-all(s16[8,272,128]{2,1,0:T(8,128)(2,1)S(1)} %get-tuple-element.42), channel_id=1, replica_groups=mesh['z'=8,'yh'=2,'core'=2,'x'=4,'yl'=2] {'z'}, dimensions={0} | all-to-all | bytes 1114112 | tf_op jit(solution)/shard_map/all_to_all | solution.py:384
  151.6 3.6 %forward.3 = s16[8,272,128]{2,1,0:T(8,128)(2,1)S(1)} custom-call(s32[5,16]{1,0:T(8,128)S(1)} %pad_add_fusion.meta_ref, s16[8,272,128]{2,1,0:T(8,128)(2,1)S(1)} %all_to_all.50.msg_ref, bf16[12,256,256]{2,1,0:T(8,128)(2,1)S(1)} %bitcast.37, bf16[12,256,256]{2,1,0:T(8,128)(2,1)S(1)} %copy-done.3, bf16[12,256,256]{2,1,0:T(8,128)(2,1)S(1)} %collective-permute-done.6.refs_2_, ...), custom_call_target="tpu_custom_call" | custom-call | flops 1610612736 | bytes 6291456 | tf_op jit(solution)/shard_map/forward/pallas_call | solution.py:236
  156.1 3.5 %all-to-all-start.7 = ((s16[8,272,128]{2,1,0:T(8,128)(2,1)}), s16[8,272,128]{2,1,0:T(8,128)(2,1)S(1)}, u32[]{:S(2)}, u32[]{:S(2)}) async-start(s16[8,272,128]{2,1,0:T(8,128)(2,1)} %copy-done.5), calls=%async_computation.7 | async-start | bytes 1114112 | tf_op jit(solution)/shard_map/all_to_all | solution.py:313
  159.7 2.6 %collective-permute-start.9 = (f32[264,128]{1,0:T(8,128)S(1)}, f32[264,128]{1,0:T(8,128)S(1)}, u32[]{:S(2)}, u32[]{:S(2)}) collective-permute-start(f32[264,128]{1,0:T(8,128)S(1)} %concatenate.73), channel_id=1, source_target_pairs={{0,16},{16,0},{1,17},{17,1},{2,18},{18,2},{3,19},{19,3},{4,20},{20... | collective-permute-start | bytes 405512 | tf_op jit(solution)/shard_map/ppermute | solution.py:360
  162.4 4.5 %all-to-all-done.7.msg_ref = s16[8,272,128]{2,1,0:T(8,128)(2,1)S(1)} async-done(((s16[8,272,128]{2,1,0:T(8,128)(2,1)}), s16[8,272,128]{2,1,0:T(8,128)(2,1)S(1)}, u32[]{:S(2)}, u32[]{:S(2)}) %all-to-all-start.7) | async-done | bytes 557088 | tf_op jit(solution)/shard_map/all_to_all | solution.py:313
  167.7 6.8 %all-to-all-start.8 = ((f32[128,2,128]{2,1,0:T(2,128)}), f32[128,2,128]{2,1,0:T(2,128)S(1)}, u32[]{:S(2)}, u32[]{:S(2)}) async-start(f32[128,2,128]{2,1,0:T(2,128)} %last_end.1), calls=%async_computation.8 | async-start | bytes 262144 | tf_op jit(solution)/shard_map/all_to_all | solution.py:345
  174.7 9.8 %collective-permute-start.10 = (f32[136,256]{1,0:T(8,128)S(1)}, f32[136,256]{1,0:T(8,128)S(1)}, u32[]{:S(2)}, u32[]{:S(2)}) collective-permute-start(f32[136,256]{1,0:T(8,128)S(1)} %pad_maximum_fusion), channel_id=1, source_target_pairs={{0,8},{8,0},{1,9},{9,1},{2,10},{10,2},{3,11},{11,3},{4,12},{12,4},... | collective-permute-start | bytes 417800 | tf_op jit(solution)/shard_map/ppermute | solution.py:360
  184.5 1.5 all-to-all-done.8
  186.1 10.9 %collective-permute-start.11 = (f32[2,256]{1,0:T(2,128)S(1)}, f32[2,256]{1,0:T(2,128)S(1)}, u32[]{:S(2)}, u32[]{:S(2)}) collective-permute-start(f32[2,256]{1,0:T(2,128)S(1)} %pad_maximum_fusion.2), channel_id=1, source_target_pairs={{0,8},{8,0},{1,9},{9,1},{2,10},{10,2},{3,11},{11,3},{4,12},{12,4},... | collective-permute-start | bytes 6152 | tf_op jit(solution)/shard_map/ppermute | solution.py:347
  (78 shorter events, 11.3 us)
Async XLA Ops:
  0.6 22.0 %copy-start = (bf16[1,1,12,256,256]{4,3,2,1,0:T(8,128)(2,1)S(1)}, bf16[1,1,12,256,256]{4,3,2,1,0:T(8,128)(2,1)}, u32[]{:S(2)}) copy-start(bf16[1,1,12,256,256]{4,3,2,1,0:T(8,128)(2,1)} %param.5) | copy-start | bytes 4718596
  0.6 12.3 %copy-start.10 = (s32[1,1,12]{2,1,0:T(1,128)S(1)}, s32[1,1,12]{2,1,0:T(1,128)}, u32[]{:S(2)}) copy-start(s32[1,1,12]{2,1,0:T(1,128)} %param.6) | copy-start | bytes 148
  0.6 21.9 %collective-permute-start.4 = (bf16[12,256,256]{2,1,0:T(8,128)(2,1)}, bf16[12,256,256]{2,1,0:T(8,128)(2,1)S(1)}, u32[]{:S(2)}, u32[]{:S(2)}) collective-permute-start(bf16[12,256,256]{2,1,0:T(8,128)(2,1)} %bitcast.31), channel_id=1, source_target_pairs={{0,8},{8,0},{1,9},{9,1},{2,10},{10,2},{3,11},{11,3},{4,12},{12,4},... | collective-permute-start | bytes 4718600 | tf_op jit(solution)/shard_map/ppermute | solution.py:273
  4.9 2.2 %collective-permute-start.1 = (f32[64,256]{1,0:T(8,128)S(1)}, f32[64,256]{1,0:T(8,128)S(1)}, u32[]{:S(2)}, u32[]{:S(2)}) collective-permute-start(f32[64,256]{1,0:T(8,128)S(1)} %get-tuple-element.58), channel_id=1, source_target_pairs={{0,8},{8,0},{1,9},{9,1},{2,10},{10,2},{3,11},{11,3},{4,12},{12,4},... | collective-permute-start | bytes 196616 | tf_op jit(solution)/shard_map/ppermute | solution.py:265
  7.3 0.8 copy-start.4
  8.1 14.5 %all-to-all-start = ((s16[8,144,256]{2,1,0:T(8,128)(2,1)}), s16[8,144,256]{2,1,0:T(8,128)(2,1)}, u32[]{:S(2)}, u32[]{:S(2)}) async-start(s16[8,144,256]{2,1,0:T(8,128)(2,1)} %copy-done.4), calls=%async_computation | async-start | bytes 1179648 | tf_op jit(solution)/shard_map/all_to_all | solution.py:374
  13.0 2.6 %collective-permute-start = (s32[16]{0:T(128)S(1)}, s32[16]{0:T(128)S(1)}, u32[]{:S(2)}, u32[]{:S(2)}) collective-permute-start(s32[16]{0:T(128)S(1)} %pad_add_fusion.2), channel_id=1, source_target_pairs={{0,8},{8,0},{1,9},{9,1},{2,10},{10,2},{3,11},{11,3},{4,12},{12,4},... | collective-permute-start | bytes 200 | tf_op jit(solution)/shard_map/ppermute | solution.py:274
  13.5 12.0 %copy-start.8 = (s32[16]{0:T(128)}, s32[16]{0:T(128)S(1)}, u32[]{:S(2)}) copy-start(s32[16]{0:T(128)S(1)} %concatenate.64) | copy-start | bytes 196
  13.6 9.0 %collective-permute-start.3 = (f32[128,128]{1,0:T(8,128)S(1)}, f32[128,128]{1,0:T(8,128)S(1)}, u32[]{:S(2)}, u32[]{:S(2)}) collective-permute-start(f32[128,128]{1,0:T(8,128)S(1)} %get-tuple-element.56), channel_id=1, source_target_pairs={{0,16},{16,0},{1,17},{17,1},{2,18},{18,2},{3,19},{19,3},{4,20},{20... | collective-permute-start | bytes 196616 | tf_op jit(solution)/shard_map/ppermute | solution.py:272
  15.6 6.9 %collective-permute-start.2 = (s32[2,16]{1,0:T(2,128)S(1)}, s32[2,16]{1,0:T(2,128)S(1)}, u32[]{:S(2)}, u32[]{:S(2)}) collective-permute-start(s32[2,16]{1,0:T(2,128)S(1)} %pad_add_fusion.1), channel_id=1, source_target_pairs={{0,16},{16,0},{1,17},{17,1},{2,18},{18,2},{3,19},{19,3},{4,20},{20... | collective-permute-start | bytes 392 | tf_op jit(solution)/shard_map/ppermute | solution.py:275
  22.6 2.9 %copy-start.11 = (s32[2,16]{1,0:T(2,128)}, s32[2,16]{1,0:T(2,128)S(1)}, u32[]{:S(2)}) copy-start(s32[2,16]{1,0:T(2,128)S(1)} %collective-permute-done.2) | copy-start | bytes 388
  22.6 4.3 %copy-start.1 = (bf16[12,256,256]{2,1,0:T(8,128)(2,1)}, bf16[12,256,256]{2,1,0:T(8,128)(2,1)S(1)}, u32[]{:S(2)}) copy-start(bf16[12,256,256]{2,1,0:T(8,128)(2,1)S(1)} %collective-permute-done.4.refs_1_) | copy-start | bytes 4718596
  25.5 14.9 %collective-permute-start.5 = (s16[8,272,128]{2,1,0:T(8,128)(2,1)S(1)}, s16[8,272,128]{2,1,0:T(8,128)(2,1)S(1)}, u32[]{:S(2)}, u32[]{:S(2)}) collective-permute-start(s16[8,272,128]{2,1,0:T(8,128)(2,1)S(1)} %sent_adjoint.1), channel_id=1, source_target_pairs={{0,16},{16,0},{1,17},{17,1},{2,18},{18,2},{3,19},{19,3},{4,20},{20... | collective-permute-start | bytes 1671176 | tf_op jit(solution)/shard_map/ppermute | solution.py:292
  40.4 35.7 %collective-permute-start.6 = (bf16[12,256,256]{2,1,0:T(8,128)(2,1)S(1)}, bf16[12,256,256]{2,1,0:T(8,128)(2,1)S(1)}, u32[]{:S(2)}, u32[]{:S(2)}) collective-permute-start(bf16[12,256,256]{2,1,0:T(8,128)(2,1)S(1)} %bitcast.34), channel_id=1, source_target_pairs={{0,16},{16,0},{1,17},{17,1},{2,18},{18,2},{3,19},{19,3},{4,20},{20... | collective-permute-start | bytes 4718600 | tf_op jit(solution)/shard_map/ppermute | solution.py:294
  41.5 0.8 copy-start.6
  42.3 23.7 %all-to-all-start.1 = ((s16[8,272,128]{2,1,0:T(8,128)(2,1)}), s16[8,272,128]{2,1,0:T(8,128)(2,1)}, u32[]{:S(2)}, u32[]{:S(2)}) async-start(s16[8,272,128]{2,1,0:T(8,128)(2,1)} %copy-done.6), calls=%async_computation.1 | async-start | bytes 1114112 | tf_op jit(solution)/shard_map/all_to_all | solution.py:379
  67.4 0.8 copy-start.7
  68.2 19.1 %all-to-all-start.2 = ((s16[8,272,128]{2,1,0:T(8,128)(2,1)}), s16[8,272,128]{2,1,0:T(8,128)(2,1)}, u32[]{:S(2)}, u32[]{:S(2)}) async-start(s16[8,272,128]{2,1,0:T(8,128)(2,1)} %copy-done.7), calls=%async_computation.2 | async-start | bytes 1114112 | tf_op jit(solution)/shard_map/all_to_all | solution.py:384
  72.4 7.6 %copy-start.9 = (s32[16]{0:T(128)S(1)}, s32[16]{0:T(128)}, u32[]{:S(2)}) copy-start(s32[16]{0:T(128)} %copy-done.8) | copy-start | bytes 196
  72.4 7.6 %copy-start.12 = (s32[2,16]{1,0:T(2,128)S(1)}, s32[2,16]{1,0:T(2,128)}, u32[]{:S(2)}) copy-start(s32[2,16]{1,0:T(2,128)} %copy-done.11) | copy-start | bytes 388
  77.4 10.0 %collective-permute-start.8 = (bf16[6,256,256]{2,1,0:T(8,128)(2,1)}, bf16[6,256,256]{2,1,0:T(8,128)(2,1)}, u32[]{:S(2)}, u32[]{:S(2)}) collective-permute-start(bf16[6,256,256]{2,1,0:T(8,128)(2,1)} %get-tuple-element.46), channel_id=1, source_target_pairs={{0,8},{8,0},{1,9},{9,1},{2,10},{10,2},{3,11},{11,3},{4,12},{12,4},... | collective-permute-start | bytes 2359304 | tf_op jit(solution)/shard_map/ppermute | solution.py:381
  80.0 7.3 %collective-permute-start.7 = (bf16[6,256,256]{2,1,0:T(8,128)(2,1)}, bf16[6,256,256]{2,1,0:T(8,128)(2,1)}, u32[]{:S(2)}, u32[]{:S(2)}) collective-permute-start(bf16[6,256,256]{2,1,0:T(8,128)(2,1)} %get-tuple-element.47), channel_id=1, source_target_pairs={{0,8},{8,0},{1,9},{9,1},{2,10},{10,2},{3,11},{11,3},{4,12},{12,4},... | collective-permute-start | bytes 2359304 | tf_op jit(solution)/shard_map/ppermute | solution.py:381
  87.3 1.4 copy-start.2
  92.6 25.1 %copy-start.3 = (bf16[12,256,256]{2,1,0:T(8,128)(2,1)S(1)}, bf16[12,256,256]{2,1,0:T(8,128)(2,1)}, u32[]{:S(2)}) copy-start(bf16[12,256,256]{2,1,0:T(8,128)(2,1)} %copy-done.1) | copy-start | bytes 4718596
  155.2 0.8 copy-start.5
  156.1 10.8 %all-to-all-start.7 = ((s16[8,272,128]{2,1,0:T(8,128)(2,1)}), s16[8,272,128]{2,1,0:T(8,128)(2,1)S(1)}, u32[]{:S(2)}, u32[]{:S(2)}) async-start(s16[8,272,128]{2,1,0:T(8,128)(2,1)} %copy-done.5), calls=%async_computation.7 | async-start | bytes 1114112 | tf_op jit(solution)/shard_map/all_to_all | solution.py:313
  159.7 14.8 %collective-permute-start.9 = (f32[264,128]{1,0:T(8,128)S(1)}, f32[264,128]{1,0:T(8,128)S(1)}, u32[]{:S(2)}, u32[]{:S(2)}) collective-permute-start(f32[264,128]{1,0:T(8,128)S(1)} %concatenate.73), channel_id=1, source_target_pairs={{0,16},{16,0},{1,17},{17,1},{2,18},{18,2},{3,19},{19,3},{4,20},{20... | collective-permute-start | bytes 405512 | tf_op jit(solution)/shard_map/ppermute | solution.py:360
  167.7 18.2 %all-to-all-start.8 = ((f32[128,2,128]{2,1,0:T(2,128)}), f32[128,2,128]{2,1,0:T(2,128)S(1)}, u32[]{:S(2)}, u32[]{:S(2)}) async-start(f32[128,2,128]{2,1,0:T(2,128)} %last_end.1), calls=%async_computation.8 | async-start | bytes 262144 | tf_op jit(solution)/shard_map/all_to_all | solution.py:345
  174.7 22.3 %collective-permute-start.10 = (f32[136,256]{1,0:T(8,128)S(1)}, f32[136,256]{1,0:T(8,128)S(1)}, u32[]{:S(2)}, u32[]{:S(2)}) collective-permute-start(f32[136,256]{1,0:T(8,128)S(1)} %pad_maximum_fusion), channel_id=1, source_target_pairs={{0,8},{8,0},{1,9},{9,1},{2,10},{10,2},{3,11},{11,3},{4,12},{12,4},... | collective-permute-start | bytes 417800 | tf_op jit(solution)/shard_map/ppermute | solution.py:360
  186.1 11.7 %collective-permute-start.11 = (f32[2,256]{1,0:T(2,128)S(1)}, f32[2,256]{1,0:T(2,128)S(1)}, u32[]{:S(2)}, u32[]{:S(2)}) collective-permute-start(f32[2,256]{1,0:T(2,128)S(1)} %pad_maximum_fusion.2), channel_id=1, source_target_pairs={{0,8},{8,0},{1,9},{9,1},{2,10},{10,2},{3,11},{11,3},{4,12},{12,4},... | collective-permute-start | bytes 6152 | tf_op jit(solution)/shard_map/ppermute | solution.py:347
